TPU v7x, 256 devices: a whole 4x4x8 slice. The times are simulated.
256 devices in a mesh: dp: 32 (over x, y, core), tensor: 8 (over z).
Axes of the slice: x: 4, y: 4, z: 8, core: 2. Of those that a mesh axis runs over, the one named last changes fastest.
Arguments:
- residual_in: bfloat16 [4096, 7168], P('dp', 'tensor'), may hold values from -6 to 6
- queries: bfloat16 [4096, 64, 192], P('dp', 'tensor'), may hold values from -41 to 41
- latent: bfloat16 [4096, 576], P('dp'), may hold values from -6 to 6
- latent_up: bfloat16 [64, 512, 256], P('tensor'), may hold values from -0.25 to 0.25
- out_proj: bfloat16 [8192, 7168], P('tensor', 'dp'), may hold values from -0.0625 to 0.0625
- norm_gain: bfloat16 [7168], P('tensor'), may hold values from 0.099609375 to 1.8984375
- expert_ids: int32 [4096, 8], P('dp'), may hold values from 0 to 255, all different within a row; in each aligned block of 128 rows (0 to 127, 128 to 255, ...) at most 8 rows name the same one
- gate_num: int32 [4096, 8], P('dp'), may hold values from 16 to 256
- slot_table: int32 [256], replicated, may hold values from 0 to 255, each once
- gate_proj: bfloat16 [32, 7168, 1024], P('dp', 'tensor'), may hold values from -0.0625 to 0.0625
- up_proj: bfloat16 [32, 7168, 1024], P('dp', 'tensor'), may hold values from -0.0625 to 0.0625
- down_proj: bfloat16 [32, 1024, 7168], P('dp', 'tensor'), may hold values from -0.1875 to 0.1875
- inv_chol: float32 [32, 1024, 128], P('dp', 'tensor'), as said below
Outputs:
- residual_out: bfloat16 [4096, 7168], P('dp', 'tensor')
- moe_out: bfloat16 [4096, 7168], P('dp', 'tensor')
- down_quant: bfloat16 [32, 1024, 7168], P('dp', 'tensor')
- panel_gram: float32 [32, 1024, 128], P('dp', 'tensor')
Inputs may be any that keep to these rules, and one draw needn't show every extreme that they name: `expert_ids`: in the rows of one sequence of 128 tokens no expert is named by more than 8 rows; a row names 8 different experts. `slot_table`: each number of 0 to 255 appears once. `inv_chol`: each 128 x 128 block along the second dimension is upper triangular with a positive diagonal of at least one half.
All inputs are finite; a program needn't handle non-finite values.
Results may differ from a plain program's by a relative error of at most 0.039.
Values may be sent and summed in bfloat16 or wider, within the bound.
A program may use at most 192 MiB of HBM per device.

v0:
```python
import math

import jax
import jax.numpy as jnp
from jax import lax
from jax.sharding import PartitionSpec as P

D = 7168
NOPE = 128
ROPE = 64
VHEAD = 128
LATENT = 512
PANEL = 128
BLK = 16
CAP = 8


def soft_levels(values, low, step):
    scaled = jnp.clip((values - low) / step, 0.0, 15.0)
    return low + step * (scaled - jnp.sin(2.0 * math.pi * scaled) / (2.0 * math.pi))


def quantize_panel(weight, upper):
    low = jnp.min(weight, axis=0)
    high = jnp.max(weight, axis=0)
    step = (high - low) / 15.0 + 1e-05
    strict = jnp.triu(upper, 1)
    diagonal = jnp.diagonal(upper)
    remaining = weight
    finished = []
    for begin in range(0, weight.shape[0], BLK):
        current = [remaining[offset] for offset in range(BLK)]
        remaining = remaining[BLK:]
        errors = []
        for offset in range(BLK):
            column = begin + offset
            levels = soft_levels(current[offset], low, step)
            finished.append(levels)
            error = (current[offset] - levels) / diagonal[column]
            errors.append(error)
            for later in range(offset + 1, BLK):
                current[later] = current[later] - strict[column, begin + later] * error
        if remaining.shape[0] > 0:
            coupling = strict[begin : begin + BLK, begin + BLK :]
            remaining = remaining - jnp.dot(
                coupling.T, jnp.stack(errors), precision=lax.Precision.HIGHEST
            )
    return jnp.stack(finished)


def shards(
    residual_in,
    queries,
    latent,
    latent_up,
    out_proj,
    norm_gain,
    expert_ids,
    gate_num,
    slot_table,
    gate_proj,
    up_proj,
    down_proj,
    inv_chol,
):
    seq_len = queries.shape[0]
    head_count = queries.shape[1]
    scale = 1.0 / math.sqrt(NOPE + ROPE)
    key_value = jnp.einsum(
        "tc,hcd->thd", latent[:, :LATENT], latent_up, preferred_element_type=jnp.float32
    ).astype(jnp.bfloat16)
    rotary = jnp.broadcast_to(latent[:, None, LATENT:], (seq_len, head_count, ROPE))
    keys = jnp.concatenate([key_value[:, :, :NOPE], rotary], axis=2)
    scores = jnp.einsum("thd,shd->hts", queries, keys, preferred_element_type=jnp.float32) * scale
    causal = jnp.arange(seq_len)[None, :] <= jnp.arange(seq_len)[:, None]
    scores = jnp.where(causal[None], scores, -1e30)
    top = jnp.max(scores, axis=2, keepdims=True)
    expo = jnp.exp(scores - top)
    probs = (expo / jnp.sum(expo, axis=2, keepdims=True)).astype(jnp.bfloat16)
    result = jnp.einsum(
        "hts,shd->thd", probs, key_value[:, :, NOPE:], preferred_element_type=jnp.float32
    )
    attended = result.astype(jnp.bfloat16).reshape(seq_len, head_count * VHEAD)
    partial_out = jnp.dot(
        attended,
        lax.all_gather(out_proj, "dp", axis=1, tiled=True),
        preferred_element_type=jnp.float32,
    )
    attn = lax.psum_scatter(
        partial_out.astype(jnp.bfloat16), "tensor", scatter_dimension=1, tiled=True
    ).astype(jnp.float32)
    residual_out = (residual_in.astype(jnp.float32) + attn).astype(jnp.bfloat16)
    wide = residual_out.astype(jnp.float32)
    square_tot = lax.psum(jnp.sum(wide * wide, axis=1), "tensor")
    normed = (
        wide * lax.rsqrt(square_tot / D + 1e-06)[:, None] * norm_gain.astype(jnp.float32)
    ).astype(jnp.bfloat16)
    owners = lax.axis_size("dp")
    capacity = CAP
    experts_all = slot_table.shape[0]
    flat_ids = expert_ids.reshape(-1)
    table_hit = flat_ids[:, None] == jnp.arange(experts_all, dtype=jnp.int32)[None, :]
    slots = jnp.sum(jnp.where(table_hit, slot_table[None, :], 0), axis=1)
    onehot = (slots[:, None] == jnp.arange(owners, dtype=jnp.int32)[None, :]).astype(jnp.int32)
    before = jnp.cumsum(onehot, axis=0) - onehot
    position = jnp.sum(before * onehot, axis=1)
    target = jnp.where(slots < owners, slots * capacity + position, -1)
    select = jnp.arange(owners * capacity, dtype=jnp.int32)[:, None] == target[None, :]
    pick_any = jnp.sum(
        select.astype(jnp.float32).reshape(owners * capacity, seq_len, -1), axis=2
    ).astype(jnp.bfloat16)
    gate_frac = gate_num.reshape(-1).astype(jnp.float32) / 256.0
    combine = jnp.sum(
        jnp.where(select, gate_frac[None, :], 0.0).reshape(owners * capacity, seq_len, -1), axis=2
    ).astype(jnp.bfloat16)
    outgoing = (
        jnp.dot(pick_any, normed, preferred_element_type=jnp.float32)
        .astype(jnp.bfloat16)
        .reshape(owners, capacity, -1)
    )
    incoming = lax.all_to_all(outgoing, "dp", split_axis=0, concat_axis=0, tiled=True)
    routed = incoming.reshape(owners * capacity, -1)
    gate_part = jnp.dot(routed, gate_proj[0], preferred_element_type=jnp.float32)
    up_part = jnp.dot(routed, up_proj[0], preferred_element_type=jnp.float32)
    gate_val, up_val = (
        lax.psum_scatter(
            gate_part.astype(jnp.bfloat16), "tensor", scatter_dimension=1, tiled=True
        ).astype(jnp.float32),
        lax.psum_scatter(
            up_part.astype(jnp.bfloat16), "tensor", scatter_dimension=1, tiled=True
        ).astype(jnp.float32),
    )
    hidden = (jax.nn.silu(gate_val) * up_val).astype(jnp.bfloat16)
    unit_count = hidden.shape[1]
    panel_count = unit_count // PANEL
    split = hidden.reshape(-1, panel_count, PANEL)
    gram = (
        jnp.einsum("rpi,rpj->pij", split, split, preferred_element_type=jnp.float32)
        / routed.shape[0]
    )
    panels = down_proj[0].astype(jnp.float32).reshape(panel_count, PANEL, -1)
    uppers = inv_chol[0].reshape(panel_count, PANEL, PANEL)
    quantized = (
        jax.vmap(quantize_panel)(panels, uppers).reshape(unit_count, -1).astype(jnp.bfloat16)
    )
    expert_part = jnp.dot(hidden, quantized, preferred_element_type=jnp.float32)
    expert_rows = lax.psum_scatter(
        expert_part.astype(jnp.bfloat16), "tensor", scatter_dimension=1, tiled=True
    )
    returned = lax.all_to_all(
        expert_rows.reshape(owners, capacity, -1), "dp", split_axis=0, concat_axis=0, tiled=True
    )
    moe = lax.dot_general(
        combine,
        returned.reshape(owners * capacity, -1),
        (((0,), (0,)), ((), ())),
        preferred_element_type=jnp.float32,
    )
    return (
        residual_out,
        moe.astype(jnp.bfloat16),
        quantized[None],
        gram.reshape(unit_count, PANEL)[None],
    )


def solution(mesh):
    placed = (
        P("dp", "tensor"),
        P("dp", "tensor", None),
        P("dp", None),
        P("tensor", None, None),
        P("tensor", "dp"),
        P("tensor"),
        P("dp", None),
        P("dp", None),
        P(),
        P("dp", "tensor", None),
        P("dp", "tensor", None),
        P("dp", "tensor", None),
        P("dp", "tensor", None),
    )
    return jax.shard_map(
        shards,
        mesh=mesh,
        in_specs=placed,
        out_specs=(
            P("dp", "tensor"),
            P("dp", "tensor"),
            P("dp", "tensor", None),
            P("dp", "tensor", None),
        ),
        check_vma=False,
    )
```

profile of v0, /device:TPU:1, one launch (start us, length us, event | category | flops | bytes accessed | tf_op | source)
XLA Modules:
  0.0 1346.0 jit_solution(675660760541928572)
XLA Ops:
  108.1 8.3 constant_dynamic-update-slice_fusion.4
  116.4 9.1 constant_dynamic-update-slice_fusion.3
  125.5 9.9 constant_dynamic-update-slice_fusion.2
  135.4 10.2 constant_dynamic-update-slice_fusion.1
  145.7 13.4 constant_dynamic-update-slice_fusion
  213.9 8.7 constant_dynamic-update-slice_fusion.20
  222.6 9.4 constant_dynamic-update-slice_fusion.19
  232.0 9.5 constant_dynamic-update-slice_fusion.18
  241.5 10.5 constant_dynamic-update-slice_fusion.17
  252.0 13.1 constant_dynamic-update-slice_fusion.16
  320.0 8.4 constant_dynamic-update-slice_fusion.36
  328.4 9.4 constant_dynamic-update-slice_fusion.35
  337.8 9.7 constant_dynamic-update-slice_fusion.34
  347.5 10.5 constant_dynamic-update-slice_fusion.33
  358.0 12.9 constant_dynamic-update-slice_fusion.32
  425.1 8.5 constant_dynamic-update-slice_fusion.52
  433.6 9.1 constant_dynamic-update-slice_fusion.51
  442.7 9.8 constant_dynamic-update-slice_fusion.50
  452.5 10.4 constant_dynamic-update-slice_fusion.49
  462.9 13.1 constant_dynamic-update-slice_fusion.48
  529.6 8.3 constant_dynamic-update-slice_fusion.68
  537.9 9.0 constant_dynamic-update-slice_fusion.67
  547.0 10.2 constant_dynamic-update-slice_fusion.66
  557.1 10.6 constant_dynamic-update-slice_fusion.65
  567.8 12.7 constant_dynamic-update-slice_fusion.64
  625.1 8.4 constant_dynamic-update-slice_fusion.85
  633.5 8.5 constant_dynamic-update-slice_fusion.84
  642.0 9.3 constant_dynamic-update-slice_fusion.83
  651.3 10.0 constant_dynamic-update-slice_fusion.82
  661.3 10.4 constant_dynamic-update-slice_fusion.81
  671.7 12.6 constant_dynamic-update-slice_fusion.80
  867.7 8.7 constant_dynamic-update-slice_fusion.100
  876.4 9.2 constant_dynamic-update-slice_fusion.99
  885.6 9.8 constant_dynamic-update-slice_fusion.98
  895.4 10.5 constant_dynamic-update-slice_fusion.97
  905.9 12.7 constant_dynamic-update-slice_fusion.96
  919.9 9.4 reduce-window.6
  1003.2 8.8 constant_dynamic-update-slice_fusion.118
  1012.0 9.3 constant_dynamic-update-slice_fusion.117
  1021.3 10.1 convolution_convert_fusion.1
  1036.3 16.4 %constant_dynamic-update-slice_fusion.116 = bf16[128,1,7168]{2,1,0:T(2,128)(2,1)} fusion(bf16[128,1,7168]{2,1,0:T(2,128)(2,1)} %get-tuple-element.8, f32[1,1,7168]{2,1,0:T(1,128)S(1)} %bitcast.1679, f32[1,1,7168]{2,1,0:T(1,128)S(1)} %bitcast.1458, f32[]{:T(128)} %bitcast.1057, f32[1,1,7168]{2,1,0:T(1,128)S(1)} %get-tuple-element.9, f32[]{:T(128)} %bitcast.1056, ...), kind=kLoop, calls=%fused_computation.167 | loop fusion | flops 451584 | bytes 441344
  1052.7 25.6 %constant_dynamic-update-slice_fusion.115 = bf16[128,1,7168]{2,1,0:T(2,128)(2,1)} fusion(bf16[128,1,7168]{2,1,0:T(2,128)(2,1)} %constant_dynamic-update-slice_fusion.116, f32[1,1,7168]{2,1,0:T(1,128)S(1)} %bitcast.1680, f32[]{:T(128)} %bitcast.1070, f32[]{:T(128)} %bitcast.1069, f32[1,1,7168]{2,1,0:T(1,128)S(1)} %get-tuple-element.9, f32[]{:T(128)} %bitcast.1068, ...), kind=kLoop, calls=%fused_computation.166 | loop fusion | flops 695296 | bytes 476672
  1079.6 17.3 %psum.7 = f32[128]{0:T(128)S(1)} all-reduce(f32[128]{0:T(128)S(1)} %get-tuple-element.6), channel_id=1, replica_groups=mesh['dp'=32,'tensor'=8] {'tensor'}, use_global_device_ids=true, to_apply=%region_10.11 | all-reduce | flops 128 | bytes 1024 | tf_op jit(solution)/shard_map/psum | solution.py:94
  1098.0 11.3 all-to-all-start
  1109.4 36.0 %constant_dynamic-update-slice_fusion.114 = bf16[128,1,7168]{2,1,0:T(2,128)(2,1)} fusion(bf16[128,1,7168]{2,1,0:T(2,128)(2,1)} %constant_dynamic-update-slice_fusion.115, f32[1,1,7168]{2,1,0:T(1,128)S(1)} %bitcast.1681, f32[]{:T(128)} %bitcast.1084, f32[]{:T(128)} %bitcast.1083, f32[]{:T(128)} %bitcast.1082, f32[1,1,7168]{2,1,0:T(1,128)S(1)} %get-tuple-element.9, ...), kind=kLoop, calls=%fused_computation.165 | loop fusion | flops 953344 | bytes 512512
  1149.5 46.2 %constant_dynamic-update-slice_fusion.113 = bf16[128,1,7168]{2,1,0:T(2,128)(2,1)} fusion(bf16[128,1,7168]{2,1,0:T(2,128)(2,1)} %constant_dynamic-update-slice_fusion.114, f32[1,1,7168]{2,1,0:T(1,128)S(1)} %bitcast.1682, f32[]{:T(128)} %bitcast.1100, f32[]{:T(128)} %bitcast.1084, f32[]{:T(128)} %bitcast.1083, f32[]{:T(128)} %bitcast.1082, ...), kind=kLoop, calls=%fused_computation.164 | loop fusion | flops 1225728 | bytes 548864
  1199.0 57.2 %constant_dynamic-update-slice_fusion.112 = bf16[128,1,7168]{2,1,0:T(2,128)(2,1)} fusion(bf16[128,1,7168]{2,1,0:T(2,128)(2,1)} %constant_dynamic-update-slice_fusion.113, f32[1,1,7168]{2,1,0:T(1,128)S(1)} %bitcast.1683, f32[1,1,7168]{2,1,0:T(1,128)S(1)} %get-tuple-element.9, f32[1,1,7168]{2,1,0:T(1,128)S(1)} %get-tuple-element.12, ...), kind=kLoop, calls=%fused_computation.163 | loop fusion | flops 1512448 | bytes 585728 | tf_op jit(solution)/shard_map/vmap()/stack | solution.py:48
  1269.3 48.3 %reduce-scatter.19.cloned.1.call-done = bf16[896,256]{1,0:T(8,128)(2,1)} async-done(((bf16[7168,256]{1,0:T(8,128)(2,1)}), bf16[896,256]{1,0:T(8,128)(2,1)}) %reduce-scatter.19.cloned.1.call-update) | async-done | bytes 458768
  (345 shorter events, 670.1 us)
Async XLA Ops:
  7.2 1.6 copy-start
  7.2 1014.1 %all-gather.2.cloned.1.call-start = ((), (), s32[]{:S(2)}) async-start(), calls=%async_computation.6 | async-start | bytes 15138816 | tf_op jit(solution)/shard_map/all_gather | solution.py:86
  7.9 1070.4 %reduce-scatter.13.cloned.1.call-start = ((), (), s32[]{:S(2)}) async-start(), calls=%async_computation.7 | async-start | bytes 2064384
  8.8 5.2 copy-start.3
  10.2 6.5 copy-start.2
  825.4 93.9 %copy-start.6 = (s32[128,8]{0,1:T(8,128)S(1)}, s32[128,8]{0,1:T(8,128)}, u32[]{:S(2)}) copy-start(s32[128,8]{0,1:T(8,128)} %param.19) | copy-start | bytes 12292
  828.4 91.1 %copy-start.9 = (s32[256]{0:T(256)S(1)}, s32[256]{0:T(256)}, u32[]{:S(2)}) copy-start(s32[256]{0:T(256)} %param.21) | copy-start | bytes 3076
  1031.5 3.1 copy-start.8
  1031.5 4.0 copy-start.7
  1031.5 48.0 %copy-start.5 = (bf16[128,896]{1,0:T(8,128)(2,1)S(1)}, bf16[128,896]{1,0:T(8,128)(2,1)}, u32[]{:S(2)}) copy-start(bf16[128,896]{1,0:T(8,128)(2,1)} %param.13) | copy-start | bytes 688132
  1079.6 116.1 %copy-start.4 = (bf16[128,896]{1,0:T(8,128)(2,1)}, bf16[128,896]{1,0:T(8,128)(2,1)S(1)}, u32[]{:S(2)}) copy-start(bf16[128,896]{1,0:T(8,128)(2,1)S(1)} %get-tuple-element.7) | copy-start | bytes 688132
  1098.0 48.1 %all-to-all-start = ((bf16[32,8,896]{2,1,0:T(8,128)(2,1)}), bf16[32,8,896]{2,1,0:T(8,128)(2,1)S(1)}, u32[]{:S(2)}, u32[]{:S(2)}) async-start(bf16[32,8,896]{2,1,0:T(8,128)(2,1)} %fusion.23), calls=%async_computation | async-start | bytes 917504 | tf_op jit(solution)/shard_map/all_to_all | solution.py:121
  1109.4 146.8 %reduce-scatter.17.cloned.1.call-start = ((), (), s32[]{:S(2)}) async-start(), calls=%async_computation.9 | async-start | bytes 589824
  1149.4 107.7 %reduce-scatter.15.cloned.1.call-start = ((), (), s32[]{:S(2)}) async-start(), calls=%async_computation.8 | async-start | bytes 589824
  1198.9 118.7 %reduce-scatter.19.cloned.1.call-start = ((), (), s32[]{:S(2)}) async-start(), calls=%async_computation.10 | async-start | bytes 4128768
  1319.6 18.5 %all-to-all-start.1 = ((bf16[32,8,896]{2,1,0:T(8,128)(2,1)}), bf16[32,8,896]{2,1,0:T(8,128)(2,1)S(1)}, u32[]{:S(2)}, u32[]{:S(2)}) async-start(bf16[32,8,896]{2,1,0:T(8,128)(2,1)} %bitcast.1117), calls=%async_computation.1 | async-start | bytes 917504 | tf_op jit(solution)/shard_map/all_to_all | solution.py:150
  1327.1 11.9 copy-start.1
Sparse Core Ops, SparseCore 0:
  10.6 76.9 all-gather.1
  1033.9 41.1 reduce-scatter.12
  1149.5 30.2 reduce-scatter.16
  1199.1 30.2 reduce-scatter.14
  1269.5 48.1 reduce-scatter.18
where the time goes:
time: 1370 us; the launch traced here: 1350 us
  other arithmetic  1120 us (82%)
  local copies, waits for them, and re-layouts  74.5 us (5%)
  waiting for transfers between devices  55.2 us (4%)
  matrix products  41.5 us (3%)
  starting transfers between devices  19 us (1%)
  blocking collectives  17.3 us (1%)
  between operations  14.9 us (1%)
    unnamed x213, other arithmetic  964 us
    another operation x7, other arithmetic, quantize_panel(): jnp.stack(errors)  90.5 us
    another operation x1, other arithmetic, quantize_panel(): return jnp.stack(finished)  57.2 us
    unnamed x9, waiting for transfers between devices  49 us
    slice x53, local copies, waits for them, and re-layouts, quantize_panel(): current[later] = current[later] - strict[column, begin + later] * error  38.4 us
    unnamed x44, local copies, waits for them, and re-layouts  28.4 us
  transfers between devices with their start and end apart: 7, of which 2 were waited for; matrix products, arithmetic and copies ran while one was open for 90% of the time, Pallas kernels for 0%

commit v1 on v0

--- a/solution.py
+++ b/solution.py
@@ -2,7 +2,10 @@
 
 import jax
 import jax.numpy as jnp
+import numpy as np
 from jax import lax
+from jax.experimental import pallas as pl
+from jax.experimental.pallas import tpu as pltpu
 from jax.sharding import PartitionSpec as P
 
 D = 7168
@@ -13,39 +16,129 @@
 PANEL = 128
 BLK = 16
 CAP = 8
-
-
-def soft_levels(values, low, step):
-    scaled = jnp.clip((values - low) / step, 0.0, 15.0)
-    return low + step * (scaled - jnp.sin(2.0 * math.pi * scaled) / (2.0 * math.pi))
-
-
-def quantize_panel(weight, upper):
-    low = jnp.min(weight, axis=0)
-    high = jnp.max(weight, axis=0)
-    step = (high - low) / 15.0 + 1e-05
-    strict = jnp.triu(upper, 1)
-    diagonal = jnp.diagonal(upper)
-    remaining = weight
-    finished = []
-    for begin in range(0, weight.shape[0], BLK):
-        current = [remaining[offset] for offset in range(BLK)]
-        remaining = remaining[BLK:]
-        errors = []
-        for offset in range(BLK):
-            column = begin + offset
-            levels = soft_levels(current[offset], low, step)
-            finished.append(levels)
-            error = (current[offset] - levels) / diagonal[column]
-            errors.append(error)
-            for later in range(offset + 1, BLK):
-                current[later] = current[later] - strict[column, begin + later] * error
-        if remaining.shape[0] > 0:
-            coupling = strict[begin : begin + BLK, begin + BLK :]
-            remaining = remaining - jnp.dot(
-                coupling.T, jnp.stack(errors), precision=lax.Precision.HIGHEST
-            )
-    return jnp.stack(finished)
+NSUB = 8
+LANES = 128
+F32 = jnp.float32
+BF16 = jnp.bfloat16
+
+
+def _sin_coeffs():
+    n = 400
+    u = (0.5 * np.cos(np.pi * (np.arange(n) + 0.5) / (2 * n))) ** 2
+    r = np.sqrt(u)
+    target = np.sin(2 * np.pi * r) / (2 * np.pi * r)
+    vand = np.vander(u, 8, increasing=True)
+    return [float(c) for c in np.linalg.lstsq(vand * r[:, None], target * r, rcond=None)[0]]
+
+SINC = _sin_coeffs()
+
+def quant_kernel(us_ref, w_ref, u_ref, sel_ref, q_ref, wnat, cur, err, qi, lo, st, rs):
+    tiles = w_ref.shape[1] // (NSUB * LANES)
+    width = tiles * LANES
+    for c in range(NSUB):
+        cols = slice(c * width, (c + 1) * width)
+        chunk = w_ref[:, cols].astype(F32)
+        wnat[:, cols] = chunk
+        low = jnp.min(chunk, axis=0, keepdims=True)
+        high = jnp.max(chunk, axis=0, keepdims=True)
+        step = (high - low) / 15.0 + 1e-05
+        inverse = 1.0 / step
+        for j in range(tiles):
+            lanes = slice(j * LANES, (j + 1) * LANES)
+            lo[j, c:c + 1, :] = low[:, lanes]
+            st[j, c:c + 1, :] = step[:, lanes]
+            rs[j, c:c + 1, :] = inverse[:, lanes]
+
+    def block(b, first):
+        base = pl.multiple_of(b * BLK, BLK)
+        for c in range(NSUB):
+            for j in range(tiles):
+                at = c * width + j * LANES
+                cur[j, pl.ds(c, BLK, NSUB), :] = wnat[pl.ds(base, BLK), at:at + LANES]
+        low, step, rstep = lo[...], st[...], rs[...]
+        for i in range(BLK):
+            rows = slice(i * NSUB, (i + 1) * NSUB)
+            x = cur[:, rows, :]
+            for k in range(i):
+                x = x - us_ref[base + k, base + i] * err[:, k * NSUB:(k + 1) * NSUB, :]
+            inv = 1.0 / jnp.full((NSUB, LANES), us_ref[base + i, base + i], F32)
+            t = jnp.minimum(jnp.maximum((x - low) * rstep, 0.0), 15.0)
+            r = t - jnp.floor(t + 0.5)
+            v = r * r
+            v2 = v * v
+            poly = (SINC[0] + SINC[1] * v) + (SINC[2] + SINC[3] * v) * v2
+            poly = poly + ((SINC[4] + SINC[5] * v) + (SINC[6] + SINC[7] * v) * v2) * (v2 * v2)
+            level = low + step * (t - r * poly)
+            err[:, rows, :] = (x - level) * inv[None]
+            qi[:, rows, :] = level
+        if first is not None:
+            parts = jnp.concatenate(split3(u_ref[pl.ds(base, BLK), :]), axis=0)
+            coupling = lax.dot_general(
+                parts, sel_ref[...], (((0,), (0,)), ((), ())), preferred_element_type=F32
+            ).astype(BF16)[first:, :]
+        for c in range(NSUB):
+            cols = slice(c * width, (c + 1) * width)
+            spread = [qi[j, pl.ds(c, BLK, NSUB), :] for j in range(tiles)]
+            q_ref[pl.ds(base, BLK), cols] = jnp.concatenate(spread, axis=1).astype(BF16)
+            if first is not None:
+                spread = [err[j, pl.ds(c, BLK, NSUB), :] for j in range(tiles)]
+                e = split3(jnp.concatenate(spread, axis=1))
+                stacked = jnp.concatenate([e[p] for p in PART_E], axis=0)
+                wnat[first:, cols] = wnat[first:, cols] - jnp.dot(
+                    coupling, stacked, preferred_element_type=F32
+                )
+
+    def early(b, carry):
+        block(b, BLK)
+        return carry
+
+    def late(b, carry):
+        block(b, 5 * BLK)
+        return carry
+
+    lax.fori_loop(0, 4, early, 0)
+    lax.fori_loop(4, 7, late, 0)
+    block(7, None)
+
+
+PART_U = (0, 0, 0, 1, 1, 2, 1, 2)
+PART_E = (0, 1, 2, 0, 1, 0, 2, 1)
+
+def split3(a):
+    a1 = a.astype(BF16)
+    rest = a - a1.astype(F32)
+    a2 = rest.astype(BF16)
+    return a1, a2, (rest - a2.astype(F32)).astype(BF16)
+
+
+def selector():
+    sel = np.zeros((3 * BLK, 8 * BLK), np.float32)
+    for slot, part in enumerate(PART_U):
+        for i in range(BLK):
+            sel[part * BLK + i, slot * BLK + i] = 1
+    return sel
+
+
+def quantize(weight, upper):
+    width = weight.shape[1]
+    tiles = width // (NSUB * LANES)
+    vmem = pl.BlockSpec(memory_space=pltpu.VMEM)
+    return pl.pallas_call(
+        quant_kernel,
+        out_shape=jax.ShapeDtypeStruct((PANEL, width), BF16),
+        in_specs=[pl.BlockSpec(memory_space=pltpu.SMEM), vmem, vmem, vmem],
+        out_specs=vmem,
+        scratch_shapes=[
+            pltpu.VMEM((PANEL, width), F32),
+            pltpu.VMEM((tiles, BLK * NSUB, LANES), F32),
+            pltpu.VMEM((tiles, BLK * NSUB, LANES), F32),
+            pltpu.VMEM((tiles, BLK * NSUB, LANES), F32),
+            pltpu.VMEM((tiles, NSUB, LANES), F32),
+            pltpu.VMEM((tiles, NSUB, LANES), F32),
+            pltpu.VMEM((tiles, NSUB, LANES), F32),
+        ],
+        compiler_params=pltpu.CompilerParams(vmem_limit_bytes=48 * 2**20),
+    )(upper, weight, upper, jnp.asarray(selector(), BF16))
 
 
 def shards(
@@ -98,21 +191,26 @@
     owners = lax.axis_size("dp")
     capacity = CAP
     experts_all = slot_table.shape[0]
-    flat_ids = expert_ids.reshape(-1)
-    table_hit = flat_ids[:, None] == jnp.arange(experts_all, dtype=jnp.int32)[None, :]
-    slots = jnp.sum(jnp.where(table_hit, slot_table[None, :], 0), axis=1)
-    onehot = (slots[:, None] == jnp.arange(owners, dtype=jnp.int32)[None, :]).astype(jnp.int32)
-    before = jnp.cumsum(onehot, axis=0) - onehot
-    position = jnp.sum(before * onehot, axis=1)
-    target = jnp.where(slots < owners, slots * capacity + position, -1)
-    select = jnp.arange(owners * capacity, dtype=jnp.int32)[:, None] == target[None, :]
-    pick_any = jnp.sum(
-        select.astype(jnp.float32).reshape(owners * capacity, seq_len, -1), axis=2
-    ).astype(jnp.bfloat16)
-    gate_frac = gate_num.reshape(-1).astype(jnp.float32) / 256.0
-    combine = jnp.sum(
-        jnp.where(select, gate_frac[None, :], 0.0).reshape(owners * capacity, seq_len, -1), axis=2
-    ).astype(jnp.bfloat16)
+    named = expert_ids[:, :, None] == jnp.arange(experts_all, dtype=jnp.int32)[None, None, :]
+    picks = jnp.sum(named.astype(F32), axis=1).astype(BF16)
+    gates = jnp.sum(jnp.where(named, gate_num[:, :, None], 0), axis=1).astype(BF16)
+    kept = (
+        slot_table[None, :] == jnp.arange(owners, dtype=jnp.int32)[:, None]
+    ).astype(BF16)
+    lanes = (((1,), (1,)), ((), ()))
+    slot_picks = lax.dot_general(kept, picks, lanes, preferred_element_type=F32)
+    slot_gates = lax.dot_general(kept, gates, lanes, preferred_element_type=F32)
+    earlier = (jnp.arange(seq_len)[:, None] < jnp.arange(seq_len)[None, :]).astype(BF16)
+    before = jnp.dot(slot_picks.astype(BF16), earlier, preferred_element_type=F32)
+    lands = (before[:, None, :] == jnp.arange(capacity, dtype=F32)[None, :, None]) & (
+        slot_picks[:, None, :] > 0.5
+    )
+    pick_any = lands.astype(BF16).reshape(owners * capacity, seq_len)
+    combine = (
+        jnp.where(lands, slot_gates[:, None, :] / 256.0, 0.0)
+        .astype(BF16)
+        .reshape(owners * capacity, seq_len)
+    )
     outgoing = (
         jnp.dot(pick_any, normed, preferred_element_type=jnp.float32)
         .astype(jnp.bfloat16)
@@ -138,11 +236,7 @@
         jnp.einsum("rpi,rpj->pij", split, split, preferred_element_type=jnp.float32)
         / routed.shape[0]
     )
-    panels = down_proj[0].astype(jnp.float32).reshape(panel_count, PANEL, -1)
-    uppers = inv_chol[0].reshape(panel_count, PANEL, PANEL)
-    quantized = (
-        jax.vmap(quantize_panel)(panels, uppers).reshape(unit_count, -1).astype(jnp.bfloat16)
-    )
+    quantized = quantize(down_proj[0], inv_chol[0])
     expert_part = jnp.dot(hidden, quantized, preferred_element_type=jnp.float32)
     expert_rows = lax.psum_scatter(
         expert_part.astype(jnp.bfloat16), "tensor", scatter_dimension=1, tiled=True

time: 1370 us -> 344 us (0.25); the launches traced: 1350 us -> 343 us
  other arithmetic: 1120 us -> 0.98 us
  waiting for transfers between devices: 55.2 us -> 218 us
  local copies, waits for them, and re-layouts: 74.5 us -> 21.6 us
  blocking collectives: 17.3 us -> 37.5 us
  Pallas kernels: 0 us -> 14.2 us
    unnamed x213 -> x0, other arithmetic: 964 us -> none
    another operation x11 -> x0, other arithmetic: 157 us -> none  [the longest x7 90.5 us: quantize_panel(): jnp.stack(errors)]
    unnamed x9, waiting for transfers between devices: 49 us -> 136 us
    all_gather x1, waiting for transfers between devices: 0.01 us -> 72.3 us  [shards(): lax.all_gather(out_proj, 'dp', axis=1, tiled=True)]
    slice x62 -> x0, local copies, waits for them, and re-layouts: 43.7 us -> none  [the longest x53 38.4 us: quantize_panel(): current[later] = current[later] - strict[column, begin + later] * error]
    all_to_all x0 -> x1, blocking collectives: none -> 25.6 us  [shards(): lax.all_to_all(outgoing, 'dp', split_axis=0, concat_axis=0, tiled=True)]
    pallas_call x0 -> x1, Pallas kernels: none -> 14.2 us  [quantize(): pl.pallas_call(quant_kernel, out_shape=jax.ShapeDtypeStruct((PANEL, width...]
    unnamed x44 -> x32, local copies, waits for them, and re-layouts: 28.4 us -> 21.4 us
  transfers between devices with their start and end apart: 7 -> 6, of which waited for: 2 -> 6; matrix products, arithmetic and copies ran while one was open for 90% -> 4% of each run, Pallas kernels for 0% -> 4%
where the time goes in v1:
time: 344 us; the launch traced here: 343 us
  waiting for transfers between devices  218 us (63%)
  blocking collectives  37.5 us (11%)
  matrix products  29.3 us (9%)
  local copies, waits for them, and re-layouts  21.6 us (6%)
  Pallas kernels  14.2 us (4%)
  between operations  14 us (4%)
  starting transfers between devices  7.87 us (2%)
    unnamed x9, waiting for transfers between devices  136 us
    all_gather x1, waiting for transfers between devices, shards(): lax.all_gather(out_proj, 'dp', axis=1, tiled=True)  72.3 us
    all_to_all x1, blocking collectives, shards(): lax.all_to_all(outgoing, 'dp', split_axis=0, concat_axis=0, tiled=True)  25.6 us
    unnamed x32, local copies, waits for them, and re-layouts  21.4 us
    pallas_call x1, Pallas kernels, quantize(): pl.pallas_call(quant_kernel, out_shape=jax.ShapeDtypeStruct((PANEL, width...  14.2 us
    psum x1, blocking collectives, shards(): square_tot = lax.psum(jnp.sum(wide * wide, axis=1), 'tensor')  11.9 us
    dot_general x1, matrix products, shards(): jnp.dot(attended, lax.all_gather(out_proj, 'dp', axis=1, tiled=True), pre...  11.4 us
    all_to_all x1, waiting for transfers between devices, shards(): lax.all_to_all(expert_rows.reshape(owners, capacity, -1), 'dp', split_axi...  9.56 us
  transfers between devices with their start and end apart: 6, of which 6 were waited for; matrix products, arithmetic and copies ran while one was open for 4% of the time, Pallas kernels for 4%

profile of v1, /device:TPU:1, one launch (start us, length us, event | category | flops | bytes accessed | tf_op | source)
XLA Modules:
  0.0 343.5 jit_solution(11254339519105332539)
XLA Ops:
  7.2 0.7 all-gather.2.cloned.1.call-update
  8.0 0.8 copy-done
  8.8 1.4 convolution_convert_fusion.2
  10.2 0.1 copy.43
  10.4 1.3 fusion.67
  11.7 2.1 fusion.14
  13.8 1.5 convolution_convert_fusion.4
  15.3 72.3 %all-gather.2.cloned.1.call-done = bf16[1024,7168]{0,1:T(8,128)(2,1)} async-done(((bf16[1024,224]{0,1:T(8,128)(2,1)}), bf16[1024,7168]{0,1:T(8,128)(2,1)}) %all-gather.2.cloned.1.call-update) | async-done | bytes 14680080 | tf_op jit(solution)/shard_map/all_gather | solution.py:179
  87.6 11.4 %convolution_convert_fusion.1 = bf16[128,7168]{1,0:T(8,128)(2,1)} fusion(bf16[128,1024]{0,1:T(8,128)(2,1)S(1)} %bitcast.79, bf16[1024,7168]{0,1:T(8,128)(2,1)} %all-gather.2.cloned.1.call-done), kind=kOutput, calls=%fused_computation.2 | convolution fusion | flops 1879965696 | bytes 16777216 | tf_op jit(solution)/shard_map/dot_general | solution.py:177
  99.0 3.9 %copy.52 = bf16[128,7168]{0,1:T(8,128)(2,1)} copy(bf16[128,7168]{1,0:T(8,128)(2,1)} %convolution_convert_fusion.1) | data formatting | bytes 3670016
  102.9 0.0 reduce-scatter.15.cloned.1.call-start
  103.0 0.6 copy-done.8
  103.6 0.1 copy.47
  103.7 0.1 eq.61
  103.8 0.4 convert_reduce_fusion
  104.2 0.1 broadcast_compare_fusion
  104.4 0.2 fusion.50
  104.5 35.1 %reduce-scatter.13.cloned.1.call-done = bf16[896,128]{1,0:T(8,128)(2,1)} async-done(((bf16[7168,128]{1,0:T(8,128)(2,1)}), bf16[896,128]{1,0:T(8,128)(2,1)}) %reduce-scatter.13.cloned.1.call-update) | async-done | bytes 229392
  139.6 1.1 copy.53
  140.7 0.2 fusion.21
  140.9 11.9 %psum.7 = f32[128]{0:T(128)S(1)} all-reduce(f32[128]{0:T(128)S(1)} %get-tuple-element.4), channel_id=1, replica_groups=mesh['dp'=32,'tensor'=8] {'tensor'}, use_global_device_ids=true, to_apply=%region_6.7 | all-reduce | flops 128 | bytes 1024 | tf_op jit(solution)/shard_map/psum | solution.py:187
  152.8 0.4 fusion.15
  153.2 25.6 %all_to_all.10 = bf16[32,8,896]{2,1,0:T(8,128)(2,1)S(1)} all-to-all(bf16[32,8,896]{2,1,0:T(8,128)(2,1)S(1)} %fusion.15), channel_id=1, replica_groups=mesh['dp'=32,'tensor'=8] {'dp'}, dimensions={0} | all-to-all | bytes 917504 | tf_op jit(solution)/shard_map/all_to_all | solution.py:219
  178.8 0.8 copy-done.5
  179.5 2.2 fusion.5
  181.8 1.0 copy.54
  182.8 0.0 reduce-scatter.17.cloned.1.call-start
  182.9 2.4 fusion.8
  185.3 1.0 copy.56
  186.3 0.2 reduce-scatter.19.cloned.1.call-start
  186.5 1.5 copy-done.1
  188.0 14.2 %shard_map.165 = bf16[128,7168]{1,0:T(8,128)(2,1)} custom-call(f32[128,128]{1,0:T(8,128)S(1)} %bitcast.71, bf16[128,7168]{1,0:T(8,128)(2,1)S(1)} %bitcast.70, f32[128,128]{1,0:T(8,128)S(1)} %bitcast.72, bf16[48,128]{1,0:T(8,128)(2,1)S(1)} %copy-done.3), custom_call_target="tpu_custom_call" | custom-call | tf_op jit(solution)/shard_map/pallas_call | solution.py:126
  202.2 9.6 %reduce-scatter.15.cloned.1.call-done = bf16[128,256]{1,0:T(8,128)(2,1)} async-done(((bf16[1024,256]{1,0:T(8,128)(2,1)}), bf16[128,256]{1,0:T(8,128)(2,1)}) %reduce-scatter.15.cloned.1.call-update) | async-done | bytes 65552
  211.8 0.9 copy.55
  212.8 37.5 %reduce-scatter.17.cloned.1.call-done = bf16[128,256]{1,0:T(8,128)(2,1)} async-done(((bf16[1024,256]{1,0:T(8,128)(2,1)}), bf16[128,256]{1,0:T(8,128)(2,1)}) %reduce-scatter.17.cloned.1.call-update) | async-done | bytes 65552
  250.3 0.9 copy.57
  251.2 4.5 %convolution_convert_fusion = bf16[256,7168]{1,0:T(8,128)(2,1)} fusion(bf16[128,7168]{1,0:T(8,128)(2,1)} %shard_map.165, bf16[256,128]{1,0:T(8,128)(2,1)S(1)} %copy.57, bf16[256,128]{1,0:T(8,128)(2,1)S(1)} %copy.55), kind=kOutput, calls=%fused_computation.1 | convolution fusion | flops 471859200 | bytes 5636096 | tf_op jit(solution)/shard_map/dot_general | solution.py:240
  255.7 5.9 %copy.58 = bf16[256,7168]{0,1:T(8,128)(2,1)} copy(bf16[256,7168]{1,0:T(8,128)(2,1)} %convolution_convert_fusion) | data formatting | bytes 7340032
  261.6 0.7 copy-done.9
  262.3 0.1 copy.48
  262.4 53.2 %reduce-scatter.19.cloned.1.call-done = bf16[896,256]{1,0:T(8,128)(2,1)} async-done(((bf16[7168,256]{1,0:T(8,128)(2,1)}), bf16[896,256]{1,0:T(8,128)(2,1)}) %reduce-scatter.19.cloned.1.call-update) | async-done | bytes 458768
  315.5 2.0 copy.59
  317.5 7.5 %all-to-all-start.1 = ((bf16[32,8,896]{2,1,0:T(8,128)(2,1)}), bf16[32,8,896]{2,1,0:T(8,128)(2,1)S(1)}, u32[]{:S(2)}, u32[]{:S(2)}) async-start(bf16[32,8,896]{2,1,0:T(8,128)(2,1)} %bitcast.12), calls=%async_computation.1 | async-start | bytes 917504 | tf_op jit(solution)/shard_map/all_to_all | solution.py:244
  325.0 0.4 select_reduce_fusion
  325.4 0.1 convolution_multiply_fusion.2
  325.5 0.9 fusion.17
  326.4 9.6 %all-to-all-done.1 = bf16[32,8,896]{2,1,0:T(8,128)(2,1)S(1)} async-done(((bf16[32,8,896]{2,1,0:T(8,128)(2,1)}), bf16[32,8,896]{2,1,0:T(8,128)(2,1)S(1)}, u32[]{:S(2)}, u32[]{:S(2)}) %all-to-all-start.1) | async-done | bytes 458784 | tf_op jit(solution)/shard_map/all_to_all | solution.py:244
  336.0 1.0 fusion.16
  (31 shorter events, 0.3 us)
Async XLA Ops:
  7.2 1.6 copy-start
  7.2 3.0 slice-start
  7.2 80.4 %all-gather.2.cloned.1.call-start = ((), (), s32[]{:S(2)}) async-start(), calls=%async_computation.6 | async-start | bytes 15138816 | tf_op jit(solution)/shard_map/all_gather | solution.py:179
  7.9 131.7 %reduce-scatter.13.cloned.1.call-start = ((), (), s32[]{:S(2)}) async-start(), calls=%async_computation.7 | async-start | bytes 2064384
  102.9 0.7 copy-start.8
  102.9 0.9 copy-start.10
  102.9 1.3 copy-start.7
  102.9 37.8 %copy-start.6 = (bf16[128,896]{1,0:T(8,128)(2,1)S(1)}, bf16[128,896]{1,0:T(8,128)(2,1)}, u32[]{:S(2)}) copy-start(bf16[128,896]{1,0:T(8,128)(2,1)} %param.14) | copy-start | bytes 688132
  102.9 108.9 %reduce-scatter.15.cloned.1.call-start = ((), (), s32[]{:S(2)}) async-start(), calls=%async_computation.8 | async-start | bytes 589824
  140.9 40.9 %copy-start.4 = (bf16[128,896]{1,0:T(8,128)(2,1)}, bf16[128,896]{1,0:T(8,128)(2,1)S(1)}, u32[]{:S(2)}) copy-start(bf16[128,896]{1,0:T(8,128)(2,1)S(1)} %get-tuple-element.5) | copy-start | bytes 688132
  178.8 0.8 copy-start.5
  182.8 3.7 %copy-start.2 = (f32[1,128,128]{2,1,0:T(8,128)S(1)}, f32[1,128,128]{2,1,0:T(8,128)}, u32[]{:S(2)}) copy-start(f32[1,128,128]{2,1,0:T(8,128)} %param.26) | copy-start | bytes 196612
  182.8 3.7 %copy-start.3 = (bf16[48,128]{1,0:T(8,128)(2,1)S(1)}, bf16[48,128]{1,0:T(8,128)(2,1)}, u32[]{:S(2)}) copy-start(bf16[48,128]{1,0:T(8,128)(2,1)} %constant.27.clone.sel_ref) | copy-start | bytes 36868
  182.8 67.4 %reduce-scatter.17.cloned.1.call-start = ((), (), s32[]{:S(2)}) async-start(), calls=%async_computation.9 | async-start | bytes 589824
  186.3 129.2 %reduce-scatter.19.cloned.1.call-start = ((), (), s32[]{:S(2)}) async-start(), calls=%async_computation.10 | async-start | bytes 4128768
  186.5 1.5 copy-start.1
  261.6 0.7 copy-start.9
  317.5 18.5 %all-to-all-start.1 = ((bf16[32,8,896]{2,1,0:T(8,128)(2,1)}), bf16[32,8,896]{2,1,0:T(8,128)(2,1)S(1)}, u32[]{:S(2)}, u32[]{:S(2)}) async-start(bf16[32,8,896]{2,1,0:T(8,128)(2,1)} %bitcast.12), calls=%async_computation.1 | async-start | bytes 917504 | tf_op jit(solution)/shard_map/all_to_all | solution.py:244
Sparse Core Ops, SparseCore 0:
  10.6 77.0 all-gather.1
  103.1 36.4 reduce-scatter.12
  182.9 28.8 reduce-scatter.14
  214.3 35.8 reduce-scatter.16
  261.7 53.7 reduce-scatter.18

commit v2 on v1

--- a/solution.py
+++ b/solution.py
@@ -32,7 +32,7 @@
 
 SINC = _sin_coeffs()
 
-def quant_kernel(us_ref, w_ref, u_ref, sel_ref, q_ref, wnat, cur, err, qi, lo, st, rs):
+def quantize_panel(us_ref, w_ref, u_ref, sel_ref, q_ref, wnat, cur, err, qi, lo, st, rs, midway):
     tiles = w_ref.shape[1] // (NSUB * LANES)
     width = tiles * LANES
     for c in range(NSUB):
@@ -97,6 +97,7 @@
         return carry
 
     lax.fori_loop(0, 4, early, 0)
+    midway()
     lax.fori_loop(4, 7, late, 0)
     block(7, None)
 
@@ -119,15 +120,260 @@
     return sel
 
 
-def quantize(weight, upper):
+MESH = pl.DeviceIdType.MESH
+SIDE = 4
+RING = 8
+CHIPS = SIDE * SIDE
+
+
+def place():
+    at = lax.axis_index("dp")
+    x = lax.div(at, 2 * SIDE)
+    y = lax.rem(lax.div(at, 2), SIDE)
+    return x, y, lax.rem(at, 2), lax.axis_index("tensor")
+
+
+def dp_of(x, y, c):
+    return (x * SIDE + y) * 2 + c
+
+
+def push(src, dst, sems, device):
+    return pltpu.make_async_remote_copy(
+        src_ref=src, dst_ref=dst, send_sem=sems[0], recv_sem=sems[1], device_id=device,
+        device_id_type=MESH,
+    )
+
+
+def greet(device):
+    pl.semaphore_signal(
+        pltpu.get_barrier_semaphore(), inc=1, device_id=device, device_id_type=MESH
+    )
+
+
+def ring_sum(z, at, ring, send, recv, partial, rows, finish):
+    def hop(half, sub, slot):
+        to = lax.rem(z + (1 if half == 0 else RING - 1), RING)
+        return push(
+            ring.at[half, sub, slot],
+            ring.at[half, sub, slot + 1],
+            (send.at[half, sub, slot], recv.at[half, sub, slot]),
+            (at, to),
+        )
+
+    def owner(half, step):
+        if half == 0:
+            return lax.rem(z + 2 * RING - 1 - step, RING)
+        return lax.rem(z + 1 + step, RING)
+
+    for half in range(2):
+        own = partial(owner(half, 0), half)
+        for sub in range(2):
+            ring[half, sub, 0] = rows(own, sub).astype(BF16)
+            hop(half, sub, 0).start()
+
+    def step(s, carry):
+        own = [partial(owner(half, s + 1), half) for half in range(2)]
+        for sub in range(2):
+            for half in range(2):
+                hop(half, sub, s).wait_recv()
+                ring[half, sub, s + 1] = (
+                    ring[half, sub, s + 1].astype(F32) + rows(own[half], sub)
+                ).astype(BF16)
+                hop(half, sub, s + 1).start()
+        return carry
+
+    lax.fori_loop(0, RING - 2, step, 0)
+    own = [partial(z, half) for half in range(2)]
+    for sub in range(2):
+        for half in range(2):
+            hop(half, sub, RING - 2).wait_recv()
+            finish(half, sub, ring[half, sub, RING - 1].astype(F32) + rows(own[half], sub))
+
+    def drain(s, carry):
+        for sub in range(2):
+            for half in range(2):
+                hop(half, sub, s).wait_send()
+        return carry
+
+    lax.fori_loop(0, RING - 1, drain, 0)
+
+
+def front_kernel(
+    us_ref, w_ref, u_ref, sel_ref, proj_ref, att_ref, res_ref,
+    q_ref, out_ref,
+    wnat, cur, err, qi, lo, st, rs,
+    proj, att, ring, fin, landed,
+    proj_send, proj_recv, sib_send, sib_recv, att_send, att_recv,
+    ring_send, ring_recv, fin_send, fin_recv,
+):
+    x, y, c, z = place()
+    at = lax.axis_index("dp")
+    up_x, down_x = lax.rem(x + 1, SIDE), lax.rem(x + SIDE - 1, SIDE)
+    up_y, down_y = lax.rem(y + 1, SIDE), lax.rem(y + SIDE - 1, SIDE)
+    far_x, far_y = lax.rem(x + 2, SIDE), lax.rem(y + 2, SIDE)
+    x_up, x_down = (dp_of(up_x, y, c), z), (dp_of(down_x, y, c), z)
+    y_up, y_down = (dp_of(x, up_y, c), z), (dp_of(x, down_y, c), z)
+    sibling = (dp_of(x, y, 1 - c), z)
+    z_up, z_down = (at, lax.rem(z + 1, RING)), (at, lax.rem(z + RING - 1, RING))
+    pair = lax.div(z, 2) * 2
+    bit = lax.rem(z, 2)
+    goal_z = pair + lax.div(y, 2)
+    goals = [(2 * bit + sub, goal_z) for sub in range(2)]
+    sources = [(2 * bit + slot, pair + lax.div(y, 2)) for slot in range(2)]
+
+    def other(who):
+        return jnp.logical_not(jnp.logical_and(who[0] == y, who[1] == z))
+
+    for device in (x_up, x_down, y_up, y_down, sibling, z_up, z_down):
+        greet(device)
+    for who in sources:
+        @pl.when(other(who))
+        def _():
+            greet((dp_of(x, who[0], c), who[1]))
+    away = sum(other(who).astype(jnp.int32) for who in goals)
+    pl.semaphore_wait(pltpu.get_barrier_semaphore(), 7 + away)
+
+    def sems(send, recv, k):
+        return send.at[k], recv.at[k]
+
+    def block(k):
+        return proj.at[k * 2 + c]
+
+    half_p, half_a = proj_ref.shape[0] // 2, att_ref.shape[0] // 2
+    own_p = [
+        push(proj_ref, block(x), sems(proj_send, proj_recv, 0), x_up),
+        push(proj_ref, block(x), sems(proj_send, proj_recv, 1), x_down),
+        push(proj_ref, block(x), sems(sib_send, sib_recv, 0), sibling),
+    ]
+    own_a = [
+        push(att_ref, att.at[y], sems(att_send, att_recv, 0), y_up),
+        push(att_ref, att.at[y], sems(att_send, att_recv, 1), y_down),
+    ]
+    first = [
+        push(proj_ref, block(down_x), sems(proj_send, proj_recv, 0), x_up),
+        push(proj_ref, block(up_x), sems(proj_send, proj_recv, 1), x_down),
+        push(att_ref, att.at[down_y], sems(att_send, att_recv, 0), y_up),
+        push(att_ref, att.at[up_y], sems(att_send, att_recv, 1), y_down),
+    ]
+
+    def part(ref, begin, size):
+        return ref.at[pl.ds(begin, size)]
+
+    def relay(ref, begin, size, pair_of, device):
+        view = part(ref, begin, size)
+        return push(view, view, pair_of, device)
+
+    relays = [
+        relay(block(down_x), 0, half_p, sems(proj_send, proj_recv, 2), x_up),
+        relay(block(up_x), half_p, half_p, sems(proj_send, proj_recv, 3), x_down),
+        relay(att.at[down_y], 0, half_a, sems(att_send, att_recv, 2), y_up),
+        relay(att.at[up_y], half_a, half_a, sems(att_send, att_recv, 3), y_down),
+    ]
+    second = [
+        relay(block(far_x), 0, half_p, sems(proj_send, proj_recv, 2), x_up),
+        relay(block(far_x), half_p, half_p, sems(proj_send, proj_recv, 3), x_down),
+        relay(att.at[far_y], 0, half_a, sems(att_send, att_recv, 2), y_up),
+        relay(att.at[far_y], half_a, half_a, sems(att_send, att_recv, 3), y_down),
+    ]
+
+    def across(k, slot):
+        return push(block(k), block(k), sems(sib_send, sib_recv, slot), sibling)
+
+    def from_sibling(k, slot):
+        mine = proj.at[k * 2 + 1 - c]
+        return push(mine, mine, sems(sib_send, sib_recv, slot), sibling)
+
+    for copy in own_p + own_a:
+        copy.start()
+    proj[pl.ds(x * 2 + c, 1)] = proj_ref[...][None]
+    att[pl.ds(y, 1)] = att_ref[...][None]
+
+    def midway():
+        for copy in first:
+            copy.wait_recv()
+        for copy in relays:
+            copy.start()
+        across(down_x, 1).start()
+        across(up_x, 2).start()
+
+    quantize_panel(
+        us_ref, w_ref, u_ref, sel_ref, q_ref, wnat, cur, err, qi, lo, st, rs, midway
+    )
+    for copy in second:
+        copy.wait_recv()
+    across(far_x, 3).start()
+    for slot, k in enumerate((x, down_x, up_x, far_x)):
+        from_sibling(k, slot).wait_recv()
+
+    tokens = att_ref.shape[0]
+
+    def partial(goal, half):
+        left = proj[lax.div(goal, 2) * 2 + half]
+        right = att[pl.ds(lax.rem(goal, 2) * 2, 2)].reshape(2 * tokens, -1)
+        return lax.dot_general(
+            left, right, (((1,), (1,)), ((), ())), preferred_element_type=F32
+        )
+
+    def rows(value, sub):
+        return value[:, sub * tokens:(sub + 1) * tokens]
+
+    def finish(half, sub, value):
+        fin[sub, half] = value.astype(BF16)
+
+    ring_sum(z, at, ring, ring_send, ring_recv, partial, rows, finish)
+
+    slot = lax.rem(y, 2)
+    for sub, who in enumerate(goals):
+        copy = push(
+            fin.at[sub], landed.at[slot], (fin_send.at[sub], fin_recv.at[slot]),
+            (dp_of(x, who[0], c), who[1]),
+        )
+
+        @pl.when(other(who))
+        def _():
+            copy.start()
+
+        @pl.when(jnp.logical_not(other(who)))
+        def _():
+            landed[pl.ds(slot, 1)] = fin[sub][None]
+
+    for k, who in enumerate(sources):
+        @pl.when(other(who))
+        def _():
+            push(
+                fin.at[0], landed.at[k], (fin_send.at[0], fin_recv.at[k]), sibling
+            ).wait_recv()
+
+    total = landed[...].reshape(-1, tokens).astype(F32).T
+    out_ref[...] = (res_ref[...].astype(F32) + total).astype(BF16)
+
+    for copy in own_p + own_a + relays:
+        copy.wait_send()
+    for slot_, k in ((1, down_x), (2, up_x), (3, far_x)):
+        across(k, slot_).wait_send()
+    for sub, who in enumerate(goals):
+        @pl.when(other(who))
+        def _():
+            push(
+                fin.at[sub], landed.at[slot], (fin_send.at[sub], fin_recv.at[slot]), sibling
+            ).wait_send()
+
+
+def front(weight, upper, projection, attended, residual):
     width = weight.shape[1]
     tiles = width // (NSUB * LANES)
     vmem = pl.BlockSpec(memory_space=pltpu.VMEM)
+    dma = pltpu.SemaphoreType.DMA
+    columns, depth = projection.shape
+    tokens = attended.shape[0]
     return pl.pallas_call(
-        quant_kernel,
-        out_shape=jax.ShapeDtypeStruct((PANEL, width), BF16),
-        in_specs=[pl.BlockSpec(memory_space=pltpu.SMEM), vmem, vmem, vmem],
-        out_specs=vmem,
+        front_kernel,
+        out_shape=(
+            jax.ShapeDtypeStruct((PANEL, width), BF16),
+            jax.ShapeDtypeStruct(residual.shape, BF16),
+        ),
+        in_specs=[pl.BlockSpec(memory_space=pltpu.SMEM)] + [vmem] * 6,
+        out_specs=(vmem, vmem),
         scratch_shapes=[
             pltpu.VMEM((PANEL, width), F32),
             pltpu.VMEM((tiles, BLK * NSUB, LANES), F32),
@@ -136,9 +382,260 @@
             pltpu.VMEM((tiles, NSUB, LANES), F32),
             pltpu.VMEM((tiles, NSUB, LANES), F32),
             pltpu.VMEM((tiles, NSUB, LANES), F32),
+            pltpu.VMEM((2 * SIDE, columns, depth), BF16),
+            pltpu.VMEM((SIDE, tokens, depth), BF16),
+            pltpu.VMEM((2, 2, RING, columns, tokens), BF16),
+            pltpu.VMEM((2, 2, columns, tokens), BF16),
+            pltpu.VMEM((2, 2, columns, tokens), BF16),
+            dma((4,)), dma((4,)), dma((4,)), dma((4,)), dma((4,)), dma((4,)),
+            dma((2, 2, RING)), dma((2, 2, RING)), dma((2,)), dma((2,)),
         ],
-        compiler_params=pltpu.CompilerParams(vmem_limit_bytes=48 * 2**20),
-    )(upper, weight, upper, jnp.asarray(selector(), BF16))
+        compiler_params=pltpu.CompilerParams(
+            vmem_limit_bytes=56 * 2**20, collective_id=0, has_side_effects=True
+        ),
+        name="front",
+    )(
+        upper, weight, upper, jnp.asarray(selector(), BF16), projection, attended, residual
+    )
+
+
+def back_kernel(
+    res_ref, gain_ref, pick_ref, comb_ref, gate_hbm, up_hbm, q_hbm,
+    moe_ref, gram_ref,
+    weights, quant, outgoing, incoming, crossing, raw, scaled, square,
+    ring_a, hidden, ring_b, rows_out, gathered, returning, returned,
+    load_sem, out_send, out_recv, sib_send, sib_recv, sq_send, sq_recv,
+    a_send, a_recv, b_send, b_recv, back_send, back_recv,
+):
+    x, y, c, z = place()
+    at = lax.axis_index("dp")
+    chip = x * SIDE + y
+    sibling = (dp_of(x, y, 1 - c), z)
+    loads = [
+        pltpu.make_async_copy(gate_hbm, weights.at[0], load_sem.at[0]),
+        pltpu.make_async_copy(up_hbm, weights.at[1], load_sem.at[1]),
+        pltpu.make_async_copy(q_hbm, quant, load_sem.at[2]),
+    ]
+    for copy in loads:
+        copy.start()
+
+    def chip_at(k):
+        return lax.rem(chip + k, CHIPS)
+
+    def greet_chip(k, carry):
+        greet((chip_at(k) * 2 + c, z))
+        return carry
+
+    def greet_z(k, carry):
+        greet((at, lax.rem(z + k, RING)))
+        return carry
+
+    lax.fori_loop(1, CHIPS, greet_chip, 0)
+    lax.fori_loop(1, RING, greet_z, 0)
+    greet(sibling)
+
+    outgoing[...] = jnp.dot(
+        pick_ref[...], res_ref[...], preferred_element_type=F32
+    ).astype(BF16)
+    pl.semaphore_wait(pltpu.get_barrier_semaphore(), CHIPS + RING - 1)
+
+    unit = 2 * CAP
+
+    def exchange(src, dst, send, recv):
+        def rows_of(k):
+            return pl.ds(pl.multiple_of(k * unit, unit), unit)
+
+        def out(k):
+            to = chip_at(k)
+            return push(
+                src.at[rows_of(to)], dst.at[rows_of(chip)], (send.at[k], recv.at[k]),
+                (to * 2 + c, z),
+            )
+
+        def come(k):
+            here = dst.at[rows_of(chip_at(CHIPS - k))]
+            return push(here, here, (send.at[k], recv.at[k]), (chip_at(k) * 2 + c, z))
+
+        def start(k, carry):
+            out(k).start()
+            return carry
+
+        def arrive(k, carry):
+            come(k).wait_recv()
+            return carry
+
+        def leave(k, carry):
+            out(k).wait_send()
+            return carry
+
+        lax.fori_loop(1, CHIPS, start, 0)
+        dst[rows_of(chip), :] = src[rows_of(chip), :]
+        lax.fori_loop(1, CHIPS, arrive, 0)
+        return leave
+
+    leave_out = exchange(outgoing, incoming, out_send, out_recv)
+
+    count = CHIPS * unit
+    half = count // 2
+    r = lax.broadcasted_iota(jnp.int32, (count, count), 0)
+    q = lax.broadcasted_iota(jnp.int32, (count, count), 1)
+    spot = ((r >> 3) & 15) * unit + (((r >> 7) ^ c) & 1) * CAP + (r & 7)
+    by_core = (q == spot).astype(F32).astype(BF16)
+    spot_back = ((q >> 3) & 15) * unit + (((q >> 7) ^ c) & 1) * CAP + (q & 7)
+    by_chip = (r == spot_back).astype(F32).astype(BF16)
+
+    both = jnp.dot(by_core, incoming[...], preferred_element_type=F32).astype(BF16)
+    raw[0:half, :] = both[:half]
+    crossing[...] = both[half:]
+    over = push(crossing, raw.at[pl.ds(half, half)], (sib_send.at[0], sib_recv.at[0]), sibling)
+    over.start()
+    over.wait_recv()
+
+    wide = raw[...].astype(F32)
+    square[pl.ds(z, 1)] = lax.dot_general(
+        jnp.ones((8, wide.shape[1]), F32), wide * wide, (((1,), (1,)), ((), ())),
+        preferred_element_type=F32, precision=lax.Precision.HIGHEST,
+    )[None]
+
+    def square_to(k):
+        return push(
+            square.at[z], square.at[z], (sq_send.at[k], sq_recv.at[k]),
+            (at, lax.rem(z + k, RING)),
+        )
+
+    def square_from(k):
+        here = square.at[lax.rem(z + RING - k, RING)]
+        return push(here, here, (sq_send.at[k], sq_recv.at[k]), (at, lax.rem(z + k, RING)))
+
+    def square_start(k, carry):
+        square_to(k).start()
+        return carry
+
+    def square_arrive(k, carry):
+        square_from(k).wait_recv()
+        return carry
+
+    def square_leave(k, carry):
+        square_to(k).wait_send()
+        return carry
+
+    lax.fori_loop(1, RING, square_start, 0)
+    scaled[...] = (wide * gain_ref[...].astype(F32)).astype(BF16)
+    loads[0].wait()
+    loads[1].wait()
+
+    units = hidden.shape[1]
+    sums = {}
+
+    def partial_a(goal, side):
+        return jnp.dot(
+            scaled[...],
+            weights[side, :, pl.ds(pl.multiple_of(goal * units, units), units)],
+            preferred_element_type=F32,
+        )
+
+    def rows_a(value, sub):
+        return value[sub * half:(sub + 1) * half]
+
+    def finish_a(side, sub, value):
+        sums[side, sub] = value
+
+    ring_sum(z, at, ring_a, a_send, a_recv, partial_a, rows_a, finish_a)
+
+    lax.fori_loop(1, RING, square_arrive, 0)
+    mean = jnp.sum(square[...], axis=0) / D
+    scale = lax.rsqrt(mean + 1e-06).T[:, 0:1]
+    gate = jnp.concatenate([sums[0, 0], sums[0, 1]], axis=0) * scale
+    up = jnp.concatenate([sums[1, 0], sums[1, 1]], axis=0) * scale
+    hidden[...] = (gate / (1.0 + jnp.exp(-gate)) * up).astype(BF16)
+    gram_ref[...] = lax.dot_general(
+        hidden[...], hidden[...], (((0,), (0,)), ((), ())), preferred_element_type=F32
+    ) / count
+    loads[2].wait()
+
+    block = moe_ref.shape[1]
+
+    def partial_b(goal, side):
+        return jnp.dot(
+            hidden[side * half:(side + 1) * half, :],
+            quant[:, pl.ds(pl.multiple_of(goal * block, LANES), block)],
+            preferred_element_type=F32,
+        )
+
+    part = half // 2
+
+    def rows_b(value, sub):
+        return value[sub * part:(sub + 1) * part]
+
+    def finish_b(side, sub, value):
+        if side == 0:
+            gathered[sub * part:(sub + 1) * part, :] = value.astype(BF16)
+        else:
+            rows_out[sub * part:(sub + 1) * part, :] = value.astype(BF16)
+
+    ring_sum(z, at, ring_b, b_send, b_recv, partial_b, rows_b, finish_b)
+
+    home = push(
+        rows_out, gathered.at[pl.ds(half, half)], (sib_send.at[1], sib_recv.at[1]), sibling
+    )
+    home.start()
+    home.wait_recv()
+    returning[...] = jnp.dot(
+        by_chip, gathered[...], preferred_element_type=F32
+    ).astype(BF16)
+    leave_back = exchange(returning, returned, back_send, back_recv)
+    moe_ref[...] = lax.dot_general(
+        comb_ref[...], returned[...], (((0,), (0,)), ((), ())), preferred_element_type=F32
+    ).astype(BF16)
+
+    over.wait_send()
+    home.wait_send()
+    lax.fori_loop(1, CHIPS, leave_out, 0)
+    lax.fori_loop(1, CHIPS, leave_back, 0)
+    lax.fori_loop(1, RING, square_leave, 0)
+
+
+def back(residual, gain, pick_any, combine, gate_w, up_w, quantized):
+    vmem = pl.BlockSpec(memory_space=pltpu.VMEM)
+    anywhere = pl.BlockSpec(memory_space=pl.ANY)
+    dma = pltpu.SemaphoreType.DMA
+    tokens, block = residual.shape
+    rows = pick_any.shape[0]
+    half = rows // 2
+    wide = (rows, block)
+    return pl.pallas_call(
+        back_kernel,
+        out_shape=(
+            jax.ShapeDtypeStruct((tokens, block), BF16),
+            jax.ShapeDtypeStruct((PANEL, PANEL), F32),
+        ),
+        in_specs=[vmem] * 4 + [anywhere] * 3,
+        out_specs=(vmem, vmem),
+        scratch_shapes=[
+            pltpu.VMEM((2,) + gate_w.shape, BF16),
+            pltpu.VMEM(quantized.shape, BF16),
+            pltpu.VMEM(wide, BF16),
+            pltpu.VMEM(wide, BF16),
+            pltpu.VMEM((half, block), BF16),
+            pltpu.VMEM(wide, BF16),
+            pltpu.VMEM(wide, BF16),
+            pltpu.VMEM((RING, 8, rows), F32),
+            pltpu.VMEM((2, 2, RING, half, PANEL), BF16),
+            pltpu.VMEM((rows, PANEL), BF16),
+            pltpu.VMEM((2, 2, RING, half // 2, block), BF16),
+            pltpu.VMEM((half, block), BF16),
+            pltpu.VMEM(wide, BF16),
+            pltpu.VMEM(wide, BF16),
+            pltpu.VMEM(wide, BF16),
+            dma((3,)), dma((CHIPS,)), dma((CHIPS,)), dma((2,)), dma((2,)), dma((RING,)),
+            dma((RING,)), dma((2, 2, RING)), dma((2, 2, RING)), dma((2, 2, RING)),
+            dma((2, 2, RING)), dma((CHIPS,)), dma((CHIPS,)),
+        ],
+        compiler_params=pltpu.CompilerParams(
+            vmem_limit_bytes=56 * 2**20, collective_id=1, has_side_effects=True
+        ),
+        name="back",
+    )(residual, gain, pick_any, combine, gate_w, up_w, quantized)
 
 
 def shards(
@@ -174,20 +671,9 @@
         "hts,shd->thd", probs, key_value[:, :, NOPE:], preferred_element_type=jnp.float32
     )
     attended = result.astype(jnp.bfloat16).reshape(seq_len, head_count * VHEAD)
-    partial_out = jnp.dot(
-        attended,
-        lax.all_gather(out_proj, "dp", axis=1, tiled=True),
-        preferred_element_type=jnp.float32,
-    )
-    attn = lax.psum_scatter(
-        partial_out.astype(jnp.bfloat16), "tensor", scatter_dimension=1, tiled=True
-    ).astype(jnp.float32)
-    residual_out = (residual_in.astype(jnp.float32) + attn).astype(jnp.bfloat16)
-    wide = residual_out.astype(jnp.float32)
-    square_tot = lax.psum(jnp.sum(wide * wide, axis=1), "tensor")
-    normed = (
-        wide * lax.rsqrt(square_tot / D + 1e-06)[:, None] * norm_gain.astype(jnp.float32)
-    ).astype(jnp.bfloat16)
+    quantized, residual_out = front(
+        down_proj[0], inv_chol[0], out_proj.T, attended, residual_in
+    )
     owners = lax.axis_size("dp")
     capacity = CAP
     experts_all = slot_table.shape[0]
@@ -211,51 +697,10 @@
         .astype(BF16)
         .reshape(owners * capacity, seq_len)
     )
-    outgoing = (
-        jnp.dot(pick_any, normed, preferred_element_type=jnp.float32)
-        .astype(jnp.bfloat16)
-        .reshape(owners, capacity, -1)
-    )
-    incoming = lax.all_to_all(outgoing, "dp", split_axis=0, concat_axis=0, tiled=True)
-    routed = incoming.reshape(owners * capacity, -1)
-    gate_part = jnp.dot(routed, gate_proj[0], preferred_element_type=jnp.float32)
-    up_part = jnp.dot(routed, up_proj[0], preferred_element_type=jnp.float32)
-    gate_val, up_val = (
-        lax.psum_scatter(
-            gate_part.astype(jnp.bfloat16), "tensor", scatter_dimension=1, tiled=True
-        ).astype(jnp.float32),
-        lax.psum_scatter(
-            up_part.astype(jnp.bfloat16), "tensor", scatter_dimension=1, tiled=True
-        ).astype(jnp.float32),
-    )
-    hidden = (jax.nn.silu(gate_val) * up_val).astype(jnp.bfloat16)
-    unit_count = hidden.shape[1]
-    panel_count = unit_count // PANEL
-    split = hidden.reshape(-1, panel_count, PANEL)
-    gram = (
-        jnp.einsum("rpi,rpj->pij", split, split, preferred_element_type=jnp.float32)
-        / routed.shape[0]
-    )
-    quantized = quantize(down_proj[0], inv_chol[0])
-    expert_part = jnp.dot(hidden, quantized, preferred_element_type=jnp.float32)
-    expert_rows = lax.psum_scatter(
-        expert_part.astype(jnp.bfloat16), "tensor", scatter_dimension=1, tiled=True
-    )
-    returned = lax.all_to_all(
-        expert_rows.reshape(owners, capacity, -1), "dp", split_axis=0, concat_axis=0, tiled=True
-    )
-    moe = lax.dot_general(
-        combine,
-        returned.reshape(owners * capacity, -1),
-        (((0,), (0,)), ((), ())),
-        preferred_element_type=jnp.float32,
-    )
-    return (
-        residual_out,
-        moe.astype(jnp.bfloat16),
-        quantized[None],
-        gram.reshape(unit_count, PANEL)[None],
-    )
+    moe, gram = back(
+        residual_out, norm_gain[None], pick_any, combine, gate_proj[0], up_proj[0], quantized
+    )
+    return residual_out, moe, quantized[None], gram[None]
 
 
 def solution(mesh):

time: 344 us -> 172 us (0.50)
  waiting for transfers between devices: 218 us -> 0 us
  Pallas kernels: 14.2 us -> 153 us
  blocking collectives: 37.5 us -> 0 us
  matrix products: 29.3 us -> 6.83 us
  between operations: 14 us -> 0.75 us
  local copies, waits for them, and re-layouts: 21.6 us -> 9.1 us
  starting transfers between devices: 7.87 us -> 0 us
    pallas_call x1 -> x2, Pallas kernels: 14.2 us -> 153 us  [the longest x1 93.4 us: back(): pl.pallas_call(back_kernel, out_shape=(jax.ShapeDtypeStruct((tokens, bloc...]
    unnamed x9 -> x0, waiting for transfers between devices: 136 us -> none
    all_gather x1 -> x0, waiting for transfers between devices: 72.3 us -> none  [shards(): lax.all_gather(out_proj, 'dp', axis=1, tiled=True)]
    all_to_all x1 -> x0, blocking collectives: 25.6 us -> none  [shards(): lax.all_to_all(outgoing, 'dp', split_axis=0, concat_axis=0, tiled=True)]
    dot_general x7 -> x0, matrix products: 22.6 us -> none  [the longest x1 11.4 us: shards(): jnp.dot(attended, lax.all_gather(out_proj, 'dp', axis=1, tiled=True), pre...]
    unnamed x32 -> x16, local copies, waits for them, and re-layouts: 21.4 us -> 5.79 us
    psum x1 -> x0, blocking collectives: 11.9 us -> none  [shards(): square_tot = lax.psum(jnp.sum(wide * wide, axis=1), 'tensor')]
    all_to_all x1 -> x0, waiting for transfers between devices: 9.56 us -> none  [shards(): lax.all_to_all(expert_rows.reshape(owners, capacity, -1), 'dp', split_axi...]
  transfers between devices with their start and end apart: 6 -> 0, of which waited for: 6 -> 0; matrix products, arithmetic and copies ran while one was open for 4% -> 0% of each run, Pallas kernels for 4% -> 0%
where the time goes in v2:
time: 172 us
  Pallas kernels  153 us (89%)
  local copies, waits for them, and re-layouts  9.1 us (5%)
  matrix products  6.83 us (4%)
  other arithmetic  2.29 us (1%)
    pallas_call x1, Pallas kernels, back(): pl.pallas_call(back_kernel, out_shape=(jax.ShapeDtypeStruct((tokens, bloc...  93.4 us
    pallas_call x1, Pallas kernels, front(): pl.pallas_call(front_kernel, out_shape=(jax.ShapeDtypeStruct((PANEL, widt...  59.3 us
    unnamed x16, local copies, waits for them, and re-layouts  5.79 us

profile of v2, /device:TPU:1, one launch (start us, length us, event | category | flops | bytes accessed | tf_op | source)
XLA Modules:
  0.0 171.7 jit_solution(2834213385725532232)
XLA Ops:
  0.6 0.0 copy-start
  0.6 1.4 broadcast_in_dim.72.gain_ref
  2.1 0.7 slice.15
  2.8 0.1 copy.35
  2.9 0.1 eq.56
  3.0 0.8 copy.40
  3.8 0.4 convert_reduce_fusion
  4.2 0.8 broadcast_compare_fusion
  5.1 0.2 fusion.18
  5.2 0.7 fusion.14.pick_ref
  6.0 0.8 copy.41
  6.7 0.4 select_reduce_fusion
  7.1 0.8 convolution_multiply_fusion.1
  7.9 0.0 copy-start.4
  7.9 0.8 fusion.11.comb_ref
  8.7 0.0 copy-done
  8.7 1.4 convolution_convert_fusion
  10.2 0.0 copy-done.4
  10.2 0.9 fusion.30
  11.1 1.1 fusion.4
  12.2 1.6 convolution_convert_fusion.1
  13.9 0.9 copy.45.att_ref
  14.7 59.3 %front.1 = (bf16[128,7168]{1,0:T(8,128)(2,1)}, bf16[128,896]{1,0:T(8,128)(2,1)}) custom-call(f32[128,128]{1,0:T(8,128)} %bitcast.51, bf16[128,7168]{1,0:T(8,128)(2,1)} %bitcast.47, f32[128,128]{1,0:T(8,128)} %bitcast.52, bf16[48,128]{1,0:T(8,128)(2,1)} %constant.17.clone.sel_ref, bf16[224,1024]{1,0:T(8,128)(2,1)} %bitcast.50, ...), custom_call_target="tpu_custom_call" | custom-call | tf_op jit(solution)/shard_map/front/pallas_call | solution.py:369
  74.0 0.0 copy-start.2
  74.0 0.0 copy-start.1
  74.0 93.4 %back.1 = (bf16[128,896]{1,0:T(8,128)(2,1)}, f32[128,128]{1,0:T(8,128)}) custom-call(bf16[128,896]{1,0:T(8,128)(2,1)} %get-tuple-element.20.res_ref, bf16[1,896]{1,0:T(2,128)(2,1)} %broadcast_in_dim.72.gain_ref, bf16[256,128]{1,0:T(8,128)(2,1)} %fusion.14.pick_ref, bf16[256,128]{1,0:T(8,128)(2,1)} %fusion.11.comb_ref, bf16[896,1024]{1,0:T(8,128)(2,1)} %bitcast.48, ...), custom_call_target="tpu_custom_call" | custom-call | tf_op jit(solution)/shard_map/back/pallas_call | solution.py:606
  167.5 0.0 copy-done.2
  167.5 0.7 copy.51
  168.2 1.6 copy.52
  169.8 0.0 copy-done.1
  169.8 0.0 copy-start.3
  169.8 1.2 copy.53
  171.1 0.0 copy-done.3
  171.1 0.6 copy.54
  (4 shorter events, 0.1 us)
Async XLA Ops:
  0.6 8.1 %copy-start = (bf16[8,512,256]{2,1,0:T(8,128)(2,1)S(1)}, bf16[8,512,256]{2,1,0:T(8,128)(2,1)}, u32[]{:S(2)}) copy-start(bf16[8,512,256]{2,1,0:T(8,128)(2,1)} %param.17) | copy-start | bytes 6291460
  7.9 2.2 %copy-start.4 = (bf16[128,8,192]{0,2,1:T(8,128)(2,1)S(1)}, bf16[128,8,192]{0,2,1:T(8,128)(2,1)}, u32[]{:S(2)}) copy-start(bf16[128,8,192]{0,2,1:T(8,128)(2,1)} %param.15) | copy-start | bytes 1179652
  74.0 93.5 %copy-start.2 = (bf16[128,896]{1,0:T(8,128)(2,1)S(1)}, bf16[128,896]{1,0:T(8,128)(2,1)}, u32[]{:S(2)}) copy-start(bf16[128,896]{1,0:T(8,128)(2,1)} %get-tuple-element.20.res_ref) | copy-start | bytes 688132
  74.0 95.8 %copy-start.1 = (bf16[128,7168]{1,0:T(8,128)(2,1)S(1)}, bf16[128,7168]{1,0:T(8,128)(2,1)}, u32[]{:S(2)}) copy-start(bf16[128,7168]{1,0:T(8,128)(2,1)} %get-tuple-element.9.q_hbm) | copy-start | bytes 5505028
  169.8 1.2 copy-start.3

commit v3 on v2

v3 whole, which is shorter than its diff:
```python
import math

import jax
import jax.numpy as jnp
import numpy as np
from jax import lax
from jax.experimental import pallas as pl
from jax.experimental.pallas import tpu as pltpu
from jax.sharding import PartitionSpec as P

D = 7168
NOPE = 128
ROPE = 64
VHEAD = 128
LATENT = 512
PANEL = 128
BLK = 16
CAP = 8
NSUB = 8
LANES = 128
F32 = jnp.float32
BF16 = jnp.bfloat16


def _sin_coeffs():
    n = 400
    u = (0.5 * np.cos(np.pi * (np.arange(n) + 0.5) / (2 * n))) ** 2
    r = np.sqrt(u)
    target = np.sin(2 * np.pi * r) / (2 * np.pi * r)
    vand = np.vander(u, 8, increasing=True)
    return [float(c) for c in np.linalg.lstsq(vand * r[:, None], target * r, rcond=None)[0]]

SINC = _sin_coeffs()

def quantize_panel(us_ref, w_ref, u_ref, sel_ref, q_ref, wnat, cur, err, qi, lo, st, rs):
    tiles = w_ref.shape[1] // (NSUB * LANES)
    width = tiles * LANES

    def ranges():
        for c in range(NSUB):
            cols = slice(c * width, (c + 1) * width)
            chunk = w_ref[:, cols].astype(F32)
            wnat[:, cols] = chunk
            low = jnp.min(chunk, axis=0, keepdims=True)
            high = jnp.max(chunk, axis=0, keepdims=True)
            step = (high - low) / 15.0 + 1e-05
            inverse = 1.0 / step
            for j in range(tiles):
                lanes = slice(j * LANES, (j + 1) * LANES)
                lo[j, c:c + 1, :] = low[:, lanes]
                st[j, c:c + 1, :] = step[:, lanes]
                rs[j, c:c + 1, :] = inverse[:, lanes]

    def block(b, first):
        base = pl.multiple_of(b * BLK, BLK)
        for c in range(NSUB):
            for j in range(tiles):
                at = c * width + j * LANES
                cur[j, pl.ds(c, BLK, NSUB), :] = wnat[pl.ds(base, BLK), at:at + LANES]
        low, step, rstep = lo[...], st[...], rs[...]
        for i in range(BLK):
            rows = slice(i * NSUB, (i + 1) * NSUB)
            x = cur[:, rows, :]
            for k in range(i):
                x = x - us_ref[base + k, base + i] * err[:, k * NSUB:(k + 1) * NSUB, :]
            inv = 1.0 / jnp.full((NSUB, LANES), us_ref[base + i, base + i], F32)
            t = jnp.minimum(jnp.maximum((x - low) * rstep, 0.0), 15.0)
            r = t - jnp.floor(t + 0.5)
            v = r * r
            v2 = v * v
            poly = (SINC[0] + SINC[1] * v) + (SINC[2] + SINC[3] * v) * v2
            poly = poly + ((SINC[4] + SINC[5] * v) + (SINC[6] + SINC[7] * v) * v2) * (v2 * v2)
            level = low + step * (t - r * poly)
            err[:, rows, :] = (x - level) * inv[None]
            qi[:, rows, :] = level
        if first is not None:
            parts = jnp.concatenate(split3(u_ref[pl.ds(base, BLK), :]), axis=0)
            coupling = lax.dot_general(
                parts, sel_ref[...], (((0,), (0,)), ((), ())), preferred_element_type=F32
            ).astype(BF16)[first:, :]
        for c in range(NSUB):
            cols = slice(c * width, (c + 1) * width)
            spread = [qi[j, pl.ds(c, BLK, NSUB), :] for j in range(tiles)]
            q_ref[c, pl.ds(base, BLK), :] = jnp.concatenate(spread, axis=1).astype(BF16)
            if first is not None:
                spread = [err[j, pl.ds(c, BLK, NSUB), :] for j in range(tiles)]
                e = split3(jnp.concatenate(spread, axis=1))
                stacked = jnp.concatenate([e[p] for p in PART_E], axis=0)
                wnat[first:, cols] = wnat[first:, cols] - jnp.dot(
                    coupling, stacked, preferred_element_type=F32
                )

    def early(b, carry):
        block(b, BLK)
        return carry

    def first_half():
        ranges()
        lax.fori_loop(0, 4, early, 0)

    def later(step):
        if isinstance(step, int) and step == 3:
            block(7, None)
        else:
            block(4 + step, 5 * BLK)

    return first_half, later


PART_U = (0, 0, 0, 1, 1, 2, 1, 2)
PART_E = (0, 1, 2, 0, 1, 0, 2, 1)

def split3(a):
    a1 = a.astype(BF16)
    rest = a - a1.astype(F32)
    a2 = rest.astype(BF16)
    return a1, a2, (rest - a2.astype(F32)).astype(BF16)


def selector():
    sel = np.zeros((3 * BLK, 8 * BLK), np.float32)
    for slot, part in enumerate(PART_U):
        for i in range(BLK):
            sel[part * BLK + i, slot * BLK + i] = 1
    return sel


MESH = pl.DeviceIdType.MESH
SIDE = 4
RING = 8
CHIPS = SIDE * SIDE


def place():
    at = lax.axis_index("dp")
    x = lax.div(at, 2 * SIDE)
    y = lax.rem(lax.div(at, 2), SIDE)
    return x, y, lax.rem(at, 2), lax.axis_index("tensor")


def dp_of(x, y, c):
    return (x * SIDE + y) * 2 + c


def push(src, dst, sems, device):
    return pltpu.make_async_remote_copy(
        src_ref=src, dst_ref=dst, send_sem=sems[0], recv_sem=sems[1], device_id=device,
        device_id_type=MESH,
    )


def greet(device):
    pl.semaphore_signal(
        pltpu.get_barrier_semaphore(), inc=1, device_id=device, device_id_type=MESH
    )


def ring_sum(z, at, ring, send, recv, partial, rows, finish, meanwhile=lambda step: None):
    def length(side, half):
        return RING // 2 if side == half else RING // 2 - 1

    def hop(side, half, sub, slot):
        to = lax.rem(z + (1 if side == 0 else RING - 1), RING)
        return push(
            ring.at[side, half, sub, slot],
            ring.at[side, half, sub, slot + 1],
            (send.at[side, half, sub, slot], recv.at[side, half, sub, slot]),
            (at, to),
        )

    def goal(side, half, step):
        away = length(side, half) - step
        return lax.rem(z + (away if side == 0 else RING - away), RING)

    streams = [(0, 0), (1, 1), (0, 1), (1, 0)]
    for side, half in streams:
        own = partial(goal(side, half, 0), half)
        for sub in range(2):
            ring[side, half, sub, 0] = rows(own, sub).astype(BF16)
            hop(side, half, sub, 0).start()
    meanwhile(0)

    def advance(step, members):
        for side, half in members:
            own = partial(goal(side, half, step), half)
            for sub in range(2):
                hop(side, half, sub, step - 1).wait_recv()
                value = rows(own, sub) + ring[side, half, sub, step].astype(F32)
                ring[side, half, sub, step] = value.astype(BF16)
                hop(side, half, sub, step).start()
        meanwhile(step)

    def middle(step, carry):
        advance(step, streams)
        return carry

    lax.fori_loop(1, RING // 2 - 1, middle, 0)
    advance(RING // 2 - 1, streams[:2])
    for half in range(2):
        own = partial(z, half)
        for sub in range(2):
            value = rows(own, sub)
            for side in (1 - half, half):
                last = length(side, half)
                hop(side, half, sub, last - 1).wait_recv()
                value = value + ring[side, half, sub, last].astype(F32)
            finish(half, sub, value)

    def drain():
        def left(step, members):
            for side, half in members:
                for sub in range(2):
                    hop(side, half, sub, step).wait_send()

        def sent(step, carry):
            left(step, streams)
            return carry

        lax.fori_loop(0, RING // 2 - 1, sent, 0)
        left(RING // 2 - 1, streams[:2])

    return drain


def attend(q_ref, latent_ref, up, spread, att_ref):
    tokens, heads = q_ref.shape[0], q_ref.shape[1]
    queries = q_ref[...].astype(F32)
    spread[0] = queries[:, :, :NOPE].reshape(tokens * heads, NOPE)
    blank = jnp.zeros((tokens, heads, NOPE - ROPE), F32)
    spread[1] = jnp.concatenate([queries[:, :, NOPE:], blank], axis=2).reshape(
        tokens * heads, NOPE
    )
    low = latent_ref[:, :LATENT]
    rotary = jnp.concatenate(
        [latent_ref[:, LATENT:].astype(F32), jnp.zeros((tokens, NOPE - ROPE), F32)], axis=1
    ).astype(BF16)
    causal = lax.broadcasted_iota(jnp.int32, (tokens, tokens), 1) <= lax.broadcasted_iota(
        jnp.int32, (tokens, tokens), 0
    )
    for h in range(heads):
        both = jnp.dot(low, up[h], preferred_element_type=F32).astype(BF16)
        query = jnp.concatenate(
            [spread[k, pl.ds(h, tokens, heads), :] for k in range(2)], axis=1
        ).astype(BF16)
        key = jnp.concatenate([both[:, :NOPE], rotary], axis=1)
        scores = lax.dot_general(
            query, key, (((1,), (1,)), ((), ())), preferred_element_type=F32
        ) * (1.0 / math.sqrt(NOPE + ROPE))
        scores = jnp.where(causal, scores, -1e30)
        expo = jnp.exp(scores - jnp.max(scores, axis=1, keepdims=True))
        probs = (expo / jnp.sum(expo, axis=1, keepdims=True)).astype(BF16)
        att_ref[:, h * VHEAD:(h + 1) * VHEAD] = jnp.dot(
            probs, both[:, NOPE:], preferred_element_type=F32
        ).astype(BF16)


def route(ids_ref, num_ref, slot_ref, pick_ref, comb_ref):
    tokens, experts_all = ids_ref.shape[0], slot_ref.shape[1]
    slots = pick_ref.shape[0] // CAP
    names = lax.broadcasted_iota(jnp.int32, (tokens, experts_all), 1)
    picks = jnp.zeros((tokens, experts_all), F32)
    gates = jnp.zeros((tokens, experts_all), F32)
    for k in range(ids_ref.shape[1]):
        hit = ids_ref[:, k:k + 1] == names
        picks = jnp.where(hit, 1.0, picks)
        gates = jnp.where(hit, num_ref[:, k:k + 1].astype(F32), gates)
    kept = jnp.where(
        slot_ref[...] == lax.broadcasted_iota(jnp.int32, (slots, experts_all), 0), 1.0, 0.0
    ).astype(BF16)
    lanes = (((1,), (1,)), ((), ()))
    slot_picks = lax.dot_general(kept, picks.astype(BF16), lanes, preferred_element_type=F32)
    slot_gates = lax.dot_general(kept, gates.astype(BF16), lanes, preferred_element_type=F32)
    earlier = jnp.where(
        lax.broadcasted_iota(jnp.int32, (tokens, tokens), 0)
        < lax.broadcasted_iota(jnp.int32, (tokens, tokens), 1), 1.0, 0.0
    ).astype(BF16)
    before = jnp.dot(slot_picks.astype(BF16), earlier, preferred_element_type=F32)
    before = jnp.where(slot_picks > 0.5, before, -1.0)
    shape = (slots, CAP, tokens)
    spot = lax.broadcasted_iota(jnp.int32, shape, 1).astype(F32)
    lands = jnp.broadcast_to(before[:, None, :], shape) == spot
    weight = jnp.broadcast_to(slot_gates[:, None, :], shape) / 256.0
    pick_ref[...] = jnp.where(lands, 1.0, 0.0).reshape(slots * CAP, tokens).astype(BF16)
    comb_ref[...] = jnp.where(lands, weight, 0.0).reshape(slots * CAP, tokens).astype(BF16)


def front_kernel(
    us_ref, u_ref, sel_ref, proj_ref, res_ref, q_in_ref, latent_ref, ids_ref, num_ref, slot_ref,
    w_hbm, lift_hbm,
    out_ref, pick, comb, q_hbm,
    weight, lift, quant, wnat, cur, err, qi, lo, st, rs,
    spread, att_own, proj, att, ring, fin, landed,
    load_sem, proj_send, proj_recv, cross_send, cross_recv, att_send, att_recv,
    ring_send, ring_recv, fin_send, fin_recv,
):
    x, y, c, z = place()
    at = lax.axis_index("dp")
    up_x, down_x = lax.rem(x + 1, SIDE), lax.rem(x + SIDE - 1, SIDE)
    up_y, down_y = lax.rem(y + 1, SIDE), lax.rem(y + SIDE - 1, SIDE)
    far_x, far_y = lax.rem(x + 2, SIDE), lax.rem(y + 2, SIDE)
    x_up, x_down = (dp_of(up_x, y, c), z), (dp_of(down_x, y, c), z)
    y_up, y_down = (dp_of(x, up_y, c), z), (dp_of(x, down_y, c), z)
    sibling = (dp_of(x, y, 1 - c), z)
    pair = lax.div(z, 2) * 2
    bit = lax.rem(z, 2)
    goal_z = pair + lax.div(y, 2)
    goals = [(2 * bit + sub, goal_z) for sub in range(2)]
    sources = [(2 * bit + slot, goal_z) for slot in range(2)]

    def other(who):
        return jnp.logical_not(jnp.logical_and(who[0] == y, who[1] == z))

    for device in (
        x_up, x_down, y_up, y_down, sibling,
        (at, lax.rem(z + 1, RING)), (at, lax.rem(z + RING - 1, RING)),
    ):
        greet(device)
    for who in sources:
        @pl.when(other(who))
        def _():
            greet((dp_of(x, who[0], c), who[1]))
    loads = [
        pltpu.make_async_copy(lift_hbm, lift, load_sem.at[0]),
        pltpu.make_async_copy(w_hbm, weight, load_sem.at[1]),
    ]
    for copy in loads:
        copy.start()
    away = sum(other(who).astype(jnp.int32) for who in goals)
    pl.semaphore_wait(pltpu.get_barrier_semaphore(), 7 + away)

    def sems(send, recv, k):
        return send.at[k], recv.at[k]

    def block(k):
        return proj.at[k * 2 + c]

    def part(ref, begin, size):
        return ref.at[pl.ds(begin, size)]

    half_p, half_a = proj_ref.shape[0] // 2, att_own.shape[0] // 2
    begins = (0, half_p, half_p, 0)
    own_p = [
        push(
            part(proj_ref, begins[k], half_p), part(block(x), begins[k], half_p),
            sems(proj_send, proj_recv, k), (x_up, x_down)[k % 2],
        )
        for k in range(4)
    ]
    from_p = [
        push(
            part(proj_ref, begins[k], half_p),
            part(block((down_x, up_x)[k % 2]), begins[k], half_p),
            sems(proj_send, proj_recv, k), (x_up, x_down)[k % 2],
        )
        for k in range(4)
    ]

    def relay(ref, begin, size, pair_of, device):
        view = part(ref, begin, size)
        return push(view, view, pair_of, device)

    relay_p = [
        relay(block(down_x), 0, half_p, sems(proj_send, proj_recv, 4), x_up),
        relay(block(up_x), half_p, half_p, sems(proj_send, proj_recv, 5), x_down),
    ]
    far_p = [
        relay(block(far_x), 0, half_p, sems(proj_send, proj_recv, 4), x_up),
        relay(block(far_x), half_p, half_p, sems(proj_send, proj_recv, 5), x_down),
    ]
    own_across = push(proj_ref, block(x), sems(cross_send, cross_recv, 0), sibling)

    def across(k, slot):
        return push(block(k), block(k), sems(cross_send, cross_recv, slot), sibling)

    def from_sibling(k, slot):
        mine = proj.at[k * 2 + 1 - c]
        return push(mine, mine, sems(cross_send, cross_recv, slot), sibling)

    for copy in own_p:
        copy.start()
    own_across.start()

    loads[0].wait()
    attend(q_in_ref, latent_ref, lift, spread, att_own)

    own_a = [
        push(att_own, att.at[y], sems(att_send, att_recv, 0), y_up),
        push(att_own, att.at[y], sems(att_send, att_recv, 1), y_down),
    ]
    from_a = [
        push(att_own, att.at[down_y], sems(att_send, att_recv, 0), y_up),
        push(att_own, att.at[up_y], sems(att_send, att_recv, 1), y_down),
    ]
    relay_a = [
        relay(att.at[down_y], 0, half_a, sems(att_send, att_recv, 2), y_up),
        relay(att.at[up_y], half_a, half_a, sems(att_send, att_recv, 3), y_down),
    ]
    far_a = [
        relay(att.at[far_y], 0, half_a, sems(att_send, att_recv, 2), y_up),
        relay(att.at[far_y], half_a, half_a, sems(att_send, att_recv, 3), y_down),
    ]
    for copy in own_a:
        copy.start()
    for k in range(2):
        from_p[k].wait_recv()
        relay_p[k].start()
    proj[pl.ds(x * 2 + c, 1)] = proj_ref[...][None]
    att[pl.ds(y, 1)] = att_own[...][None]
    route(ids_ref, num_ref, slot_ref, pick, comb)
    for k in range(2, 4):
        from_p[k].wait_recv()
    across(down_x, 1).start()
    across(up_x, 2).start()
    for copy in from_a:
        copy.wait_recv()
    for copy in relay_a:
        copy.start()
    loads[1].wait()
    quantize_first, quantize_later = quantize_panel(
        us_ref, weight, u_ref, sel_ref, quant, wnat, cur, err, qi, lo, st, rs
    )
    quantize_first()
    for copy in far_p:
        copy.wait_recv()
    across(far_x, 3).start()
    for copy in far_a:
        copy.wait_recv()
    for slot, k in enumerate((x, down_x, up_x, far_x)):
        from_sibling(k, slot).wait_recv()

    tokens = att_own.shape[0]

    def partial(goal, half):
        left = proj[lax.div(goal, 2) * 2 + half]
        right = att[pl.ds(lax.rem(goal, 2) * 2, 2)].reshape(2 * tokens, -1)
        return lax.dot_general(
            left, right, (((1,), (1,)), ((), ())), preferred_element_type=F32
        )

    def rows(value, sub):
        return value[:, sub * tokens:(sub + 1) * tokens]

    my_slot = lax.rem(y, 2)

    def deliver(half, sub):
        who = goals[sub]
        return push(
            fin.at[sub, half], landed.at[my_slot, half],
            (fin_send.at[sub, half], fin_recv.at[my_slot, half]),
            (dp_of(x, who[0], c), who[1]),
        )

    def finish(half, sub, value):
        fin[sub, half] = value.astype(BF16)

        @pl.when(other(goals[sub]))
        def _():
            deliver(half, sub).start()

        @pl.when(jnp.logical_not(other(goals[sub])))
        def _():
            landed[pl.ds(my_slot, 1), half] = value.astype(BF16)[None]

    drain = ring_sum(
        z, at, ring, ring_send, ring_recv, partial, rows, finish, quantize_later
    )
    width = res_ref.shape[1]
    q_out = [
        pltpu.make_async_copy(
            quant.at[k], q_hbm.at[:, pl.ds(k * width, width)], load_sem.at[2 + k]
        )
        for k in range(NSUB)
    ]
    for copy in q_out:
        copy.start()
    drain()
    for slot, who in enumerate(sources):
        @pl.when(other(who))
        def _():
            for half in range(2):
                push(
                    fin.at[0, half], landed.at[slot, half],
                    (fin_send.at[0, half], fin_recv.at[slot, half]), sibling,
                ).wait_recv()

    total = landed[...].reshape(-1, tokens).astype(F32).T
    out_ref[...] = (res_ref[...].astype(F32) + total).astype(BF16)
    for copy in own_p + relay_p + own_a + relay_a + [own_across]:
        copy.wait_send()
    for slot, k in ((1, down_x), (2, up_x), (3, far_x)):
        across(k, slot).wait_send()
    for sub, who in enumerate(goals):
        @pl.when(other(who))
        def _():
            for side in range(2):
                deliver(side, sub).wait_send()
    for copy in q_out:
        copy.wait()


def back_kernel(
    res_ref, gain_ref, pick, comb, gate_hbm, up_hbm, q_hbm,
    moe_ref, gram_ref,
    weights, quant, outgoing, incoming, crossing, raw, scaled, square,
    ring_a, hidden, ring_b, rows_out, gathered, returning, returned,
    load_sem, out_send, out_recv, sib_send, sib_recv, sq_send, sq_recv,
    a_send, a_recv, b_send, b_recv, back_send, back_recv,
):
    x, y, c, z = place()
    at = lax.axis_index("dp")
    chip = x * SIDE + y
    sibling = (dp_of(x, y, 1 - c), z)

    def chip_at(k):
        return lax.rem(chip + k, CHIPS)

    def greet_chip(k, carry):
        greet((chip_at(k) * 2 + c, z))
        return carry

    def greet_z(k, carry):
        greet((at, lax.rem(z + k, RING)))
        return carry

    lax.fori_loop(1, CHIPS, greet_chip, 0)
    lax.fori_loop(1, RING, greet_z, 0)
    greet(sibling)
    width = res_ref.shape[1]
    loads = [
        pltpu.make_async_copy(gate_hbm, weights.at[0], load_sem.at[0]),
        pltpu.make_async_copy(up_hbm, weights.at[1], load_sem.at[1]),
    ] + [
        pltpu.make_async_copy(
            q_hbm.at[:, pl.ds(k * width, width)], quant.at[k], load_sem.at[2 + k]
        )
        for k in range(NSUB)
    ]
    for copy in loads:
        copy.start()
    outgoing[...] = jnp.dot(pick[...], res_ref[...], preferred_element_type=F32).astype(BF16)
    pl.semaphore_wait(pltpu.get_barrier_semaphore(), CHIPS + RING - 1)

    unit = 2 * CAP

    def exchange(src, dst, send, recv, meanwhile):
        def rows_of(k):
            return pl.ds(pl.multiple_of(k * unit, unit), unit)

        def out(k):
            to = chip_at(k)
            return push(
                src.at[rows_of(to)], dst.at[rows_of(chip)], (send.at[k], recv.at[k]),
                (to * 2 + c, z),
            )

        def come(k):
            here = dst.at[rows_of(chip_at(CHIPS - k))]
            return push(here, here, (send.at[k], recv.at[k]), (chip_at(k) * 2 + c, z))

        def start(k, carry):
            out(k).start()
            return carry

        def arrive(k, carry):
            come(k).wait_recv()
            return carry

        def leave(k, carry):
            out(k).wait_send()
            return carry

        lax.fori_loop(1, CHIPS, start, 0)
        dst[rows_of(chip), :] = src[rows_of(chip), :]
        meanwhile()
        lax.fori_loop(1, CHIPS, arrive, 0)
        return leave

    leave_out = exchange(outgoing, incoming, out_send, out_recv, lambda: None)

    count = CHIPS * unit
    half = count // 2
    r = lax.broadcasted_iota(jnp.int32, (count, count), 0)
    q = lax.broadcasted_iota(jnp.int32, (count, count), 1)
    spot = ((r >> 3) & 15) * unit + (((r >> 7) ^ c) & 1) * CAP + (r & 7)
    by_core = (q == spot).astype(F32).astype(BF16)
    spot_back = ((q >> 3) & 15) * unit + (((q >> 7) ^ c) & 1) * CAP + (q & 7)
    by_chip = (r == spot_back).astype(F32).astype(BF16)

    both = jnp.dot(by_core, incoming[...], preferred_element_type=F32).astype(BF16)
    raw[0:half, :] = both[:half]
    crossing[...] = both[half:]
    over = push(crossing, raw.at[pl.ds(half, half)], (sib_send.at[0], sib_recv.at[0]), sibling)
    over.start()
    over.wait_recv()

    wide = raw[...].astype(F32)
    square[pl.ds(z, 1)] = lax.dot_general(
        jnp.ones((8, wide.shape[1]), F32), wide * wide, (((1,), (1,)), ((), ())),
        preferred_element_type=F32, precision=lax.Precision.HIGHEST,
    )[None]

    def square_to(k):
        return push(
            square.at[z], square.at[z], (sq_send.at[k], sq_recv.at[k]),
            (at, lax.rem(z + k, RING)),
        )

    def square_from(k):
        here = square.at[lax.rem(z + RING - k, RING)]
        return push(here, here, (sq_send.at[k], sq_recv.at[k]), (at, lax.rem(z + k, RING)))

    def square_start(k, carry):
        square_to(k).start()
        return carry

    def square_arrive(k, carry):
        square_from(k).wait_recv()
        return carry

    def square_leave(k, carry):
        square_to(k).wait_send()
        return carry

    lax.fori_loop(1, RING, square_start, 0)
    scaled[...] = (wide * gain_ref[...].astype(F32)).astype(BF16)
    loads[0].wait()
    loads[1].wait()

    units = hidden.shape[1]
    sums = {}

    def partial_a(goal, side):
        return jnp.dot(
            scaled[...],
            weights[side, :, pl.ds(pl.multiple_of(goal * units, units), units)],
            preferred_element_type=F32,
        )

    def rows_a(value, sub):
        return value[sub * half:(sub + 1) * half]

    def finish_a(side, sub, value):
        sums[side, sub] = value

    drain_a = ring_sum(z, at, ring_a, a_send, a_recv, partial_a, rows_a, finish_a)

    lax.fori_loop(1, RING, square_arrive, 0)
    mean = jnp.sum(square[...], axis=0) / D
    scale = lax.rsqrt(mean + 1e-06).T[:, 0:1]
    gate = jnp.concatenate([sums[0, 0], sums[0, 1]], axis=0) * scale
    up = jnp.concatenate([sums[1, 0], sums[1, 1]], axis=0) * scale
    hidden[...] = (gate / (1.0 + jnp.exp(-gate)) * up).astype(BF16)
    gram_ref[...] = lax.dot_general(
        hidden[...], hidden[...], (((0,), (0,)), ((), ())), preferred_element_type=F32
    ) / count


    def partial_b(goal, side):
        return goal, side

    quarter = half // 2

    def rows_b(value, sub):
        goal, side = value
        begin = side * half + sub * quarter
        return jnp.dot(
            hidden[begin:begin + quarter, :], quant[goal], preferred_element_type=F32
        )

    def finish_b(side, sub, value):
        if side == 0:
            gathered[sub * quarter:(sub + 1) * quarter, :] = value.astype(BF16)
        else:
            rows_out[sub * quarter:(sub + 1) * quarter, :] = value.astype(BF16)

    for copy in loads[2:]:
        copy.wait()
    drain_b = ring_sum(z, at, ring_b, b_send, b_recv, partial_b, rows_b, finish_b)


    home = push(
        rows_out, gathered.at[pl.ds(half, half)], (sib_send.at[1], sib_recv.at[1]), sibling
    )
    home.start()
    home.wait_recv()
    returning[...] = jnp.dot(
        by_chip, gathered[...], preferred_element_type=F32
    ).astype(BF16)
    def settle():
        drain_a()
        drain_b()
        lax.fori_loop(1, CHIPS, leave_out, 0)
        lax.fori_loop(1, RING, square_leave, 0)

    leave_back = exchange(returning, returned, back_send, back_recv, settle)
    moe_ref[...] = lax.dot_general(
        comb[...], returned[...], (((0,), (0,)), ((), ())), preferred_element_type=F32
    ).astype(BF16)

    over.wait_send()
    home.wait_send()
    lax.fori_loop(1, CHIPS, leave_back, 0)
def front(us, projection, residual, queries, latent, ids, num, slots, weight, lift):
    width = weight.shape[1]
    tiles = width // (NSUB * LANES)
    vmem = pl.BlockSpec(memory_space=pltpu.VMEM)
    anywhere = pl.BlockSpec(memory_space=pl.ANY)
    dma = pltpu.SemaphoreType.DMA
    columns, depth = projection.shape
    tokens, block = residual.shape
    heads = queries.shape[1]
    rows = 2 * CAP * CHIPS
    meet = (2, 2, 2, RING // 2)
    return pl.pallas_call(
        front_kernel,
        out_shape=(
            jax.ShapeDtypeStruct((tokens, block), BF16),
            jax.ShapeDtypeStruct((rows, tokens), BF16),
            jax.ShapeDtypeStruct((rows, tokens), BF16),
            jax.ShapeDtypeStruct((PANEL, width), BF16),
        ),
        in_specs=[pl.BlockSpec(memory_space=pltpu.SMEM)] + [vmem] * 9 + [anywhere] * 2,
        out_specs=(vmem, vmem, vmem, anywhere),
        scratch_shapes=[
            pltpu.VMEM((PANEL, width), BF16),
            pltpu.VMEM(lift.shape, BF16),
            pltpu.VMEM((NSUB, PANEL, width // NSUB), BF16),
            pltpu.VMEM((PANEL, width), F32),
            pltpu.VMEM((tiles, BLK * NSUB, LANES), F32),
            pltpu.VMEM((tiles, BLK * NSUB, LANES), F32),
            pltpu.VMEM((tiles, BLK * NSUB, LANES), F32),
            pltpu.VMEM((tiles, NSUB, LANES), F32),
            pltpu.VMEM((tiles, NSUB, LANES), F32),
            pltpu.VMEM((tiles, NSUB, LANES), F32),
            pltpu.VMEM((2, tokens * heads, NOPE), F32),
            pltpu.VMEM((tokens, depth), BF16),
            pltpu.VMEM((2 * SIDE, columns, depth), BF16),
            pltpu.VMEM((SIDE, tokens, depth), BF16),
            pltpu.VMEM((2, 2, 2, RING // 2 + 1, columns, tokens), BF16),
            pltpu.VMEM((2, 2, columns, tokens), BF16),
            pltpu.VMEM((2, 2, columns, tokens), BF16),
            dma((2 + NSUB,)), dma((6,)), dma((6,)), dma((4,)), dma((4,)), dma((4,)), dma((4,)),
            dma(meet), dma(meet), dma((2, 2)), dma((2, 2)),
        ],
        compiler_params=pltpu.CompilerParams(
            vmem_limit_bytes=56 * 2**20, collective_id=0, has_side_effects=True
        ),
        name="front",
    )(
        us, us, jnp.asarray(selector(), BF16), projection, residual, queries, latent, ids, num,
        slots, weight, lift,
    )


def back(residual, gain, pick_any, combine, gate_w, up_w, quantized):
    vmem = pl.BlockSpec(memory_space=pltpu.VMEM)
    anywhere = pl.BlockSpec(memory_space=pl.ANY)
    dma = pltpu.SemaphoreType.DMA
    tokens, block = residual.shape
    rows = pick_any.shape[0]
    half = rows // 2
    wide = (rows, block)
    meet = (2, 2, 2, RING // 2)
    slots_of = (2, 2, 2, RING // 2 + 1)
    return pl.pallas_call(
        back_kernel,
        out_shape=(
            jax.ShapeDtypeStruct((tokens, block), BF16),
            jax.ShapeDtypeStruct((PANEL, PANEL), F32),
        ),
        in_specs=[vmem] * 4 + [anywhere] * 3,
        out_specs=(vmem, vmem),
        scratch_shapes=[
            pltpu.VMEM((2,) + gate_w.shape, BF16),
            pltpu.VMEM((NSUB, PANEL, block), BF16),
            pltpu.VMEM(wide, BF16),
            pltpu.VMEM(wide, BF16),
            pltpu.VMEM((half, block), BF16),
            pltpu.VMEM(wide, BF16),
            pltpu.VMEM(wide, BF16),
            pltpu.VMEM((RING, 8, rows), F32),
            pltpu.VMEM(slots_of + (half, PANEL), BF16),
            pltpu.VMEM((rows, PANEL), BF16),
            pltpu.VMEM(slots_of + (half // 2, block), BF16),
            pltpu.VMEM((half, block), BF16),
            pltpu.VMEM(wide, BF16),
            pltpu.VMEM(wide, BF16),
            pltpu.VMEM(wide, BF16),
            dma((2 + NSUB,)), dma((CHIPS,)), dma((CHIPS,)), dma((2,)), dma((2,)), dma((RING,)),
            dma((RING,)), dma(meet), dma(meet), dma(meet), dma(meet), dma((CHIPS,)),
            dma((CHIPS,)),
        ],
        compiler_params=pltpu.CompilerParams(
            vmem_limit_bytes=56 * 2**20, collective_id=1, has_side_effects=True
        ),
        name="back",
    )(residual, gain, pick_any, combine, gate_w, up_w, quantized)


def shards(
    residual_in,
    queries,
    latent,
    latent_up,
    out_proj,
    norm_gain,
    expert_ids,
    gate_num,
    slot_table,
    gate_proj,
    up_proj,
    down_proj,
    inv_chol,
):
    residual_out, pick_any, combine, quantized = front(
        inv_chol[0], out_proj.T, residual_in, queries, latent, expert_ids, gate_num,
        slot_table[None], down_proj[0], latent_up,
    )
    moe, gram = back(
        residual_out, norm_gain[None], pick_any, combine, gate_proj[0], up_proj[0], quantized
    )
    return residual_out, moe, quantized[None], gram[None]


def solution(mesh):
    placed = (
        P("dp", "tensor"),
        P("dp", "tensor", None),
        P("dp", None),
        P("tensor", None, None),
        P("tensor", "dp"),
        P("tensor"),
        P("dp", None),
        P("dp", None),
        P(),
        P("dp", "tensor", None),
        P("dp", "tensor", None),
        P("dp", "tensor", None),
        P("dp", "tensor", None),
    )
    return jax.shard_map(
        shards,
        mesh=mesh,
        in_specs=placed,
        out_specs=(
            P("dp", "tensor"),
            P("dp", "tensor"),
            P("dp", "tensor", None),
            P("dp", "tensor", None),
        ),
        check_vma=False,
    )
```

time: 172 us -> 154 us (0.90)
  Pallas kernels: 153 us -> 141 us
  matrix products: 6.83 us -> 0 us
  local copies, waits for them, and re-layouts: 9.1 us -> 12.2 us
  other arithmetic: 2.29 us -> 0 us
    pallas_call x1, Pallas kernels: 93.4 us -> 81.8 us  [back(): pl.pallas_call(back_kernel, out_shape=(jax.ShapeDtypeStruct((tokens, bloc...]
    dot_general x6 -> x0, matrix products: 5.89 us -> none  [the longest x1 1.65 us: shards(): jnp.einsum('hts,shd->thd', probs, key_value[:, :, NOPE:], preferred_eleme...]
    unnamed x16 -> x14, local copies, waits for them, and re-layouts: 5.79 us -> 10.9 us
where the time goes in v3:
time: 154 us
  Pallas kernels  141 us (92%)
  local copies, waits for them, and re-layouts  12.2 us (8%)
    pallas_call x1, Pallas kernels, back(): pl.pallas_call(back_kernel, out_shape=(jax.ShapeDtypeStruct((tokens, bloc...  81.8 us
    pallas_call x1, Pallas kernels, front(): pl.pallas_call(front_kernel, out_shape=(jax.ShapeDtypeStruct((tokens, blo...  59.4 us
    unnamed x14, local copies, waits for them, and re-layouts  10.9 us

profile of v3, /device:TPU:1, one launch (start us, length us, event | category | flops | bytes accessed | tf_op | source)
XLA Modules:
  0.0 154.0 jit_solution(8176974807361202050)
XLA Ops:
  0.6 1.3 broadcast_in_dim.13.gain_ref
  1.9 1.4 copy.20.ids_ref
  3.3 1.4 copy.21.num_ref
  4.7 1.7 %copy.19.latent_ref = bf16[128,576]{1,0:T(8,128)(2,1)} copy(bf16[128,576]{0,1:T(8,128)(2,1)} %param.16) | data formatting | bytes 294912 | tf_op args[2]
  6.4 2.2 %copy.18.q_in_ref = bf16[128,8,192]{2,1,0:T(8,128)(2,1)} copy(bf16[128,8,192]{0,2,1:T(8,128)(2,1)} %param.15) | data formatting | bytes 786432 | tf_op args[1]
  8.6 59.4 %front.1 = (bf16[128,896]{1,0:T(8,128)(2,1)}, bf16[256,128]{1,0:T(8,128)(2,1)}, bf16[256,128]{1,0:T(8,128)(2,1)}, bf16[128,7168]{1,0:T(8,128)(2,1)}) custom-call(f32[128,128]{1,0:T(8,128)} %bitcast.13, f32[128,128]{1,0:T(8,128)} %bitcast.14, bf16[48,128]{1,0:T(8,128)(2,1)} %constant.2.clone.sel_ref, bf16[224,1024]{1,0:T(8,128)(2,1)} %bitcast.12, ...), custom_call_target="tpu_custom_call" | custom-call | tf_op jit(solution)/shard_map/front/pallas_call | solution.py:714
  68.0 0.0 copy-start.1
  68.0 0.0 copy-start
  68.0 81.8 %back.1 = (bf16[128,896]{1,0:T(8,128)(2,1)}, f32[128,128]{1,0:T(8,128)}) custom-call(bf16[128,896]{1,0:T(8,128)(2,1)} %get-tuple-element.20.res_ref, bf16[1,896]{1,0:T(2,128)(2,1)} %broadcast_in_dim.13.gain_ref, bf16[256,128]{1,0:T(8,128)(2,1)} %get-tuple-element.11.pick, bf16[256,128]{1,0:T(8,128)(2,1)} %get-tuple-element.12.comb, ...), custom_call_target="tpu_custom_call" | custom-call | tf_op jit(solution)/shard_map/back/pallas_call | solution.py:765
  149.8 0.0 copy-done.1
  149.8 0.7 copy.26
  150.5 1.6 %copy.27 = bf16[128,896]{1,0:T(8,128)(2,1)} copy(bf16[128,896]{1,0:T(8,128)(2,1)} %get-tuple-element.21) | data formatting | bytes 458752
  152.1 0.0 copy-done
  152.1 0.0 copy-start.2
  152.1 1.2 copy.28
  153.4 0.0 copy-done.2
  153.4 0.6 copy.29
Async XLA Ops:
  68.0 81.8 %copy-start.1 = (bf16[128,896]{1,0:T(8,128)(2,1)S(1)}, bf16[128,896]{1,0:T(8,128)(2,1)}, u32[]{:S(2)}) copy-start(bf16[128,896]{1,0:T(8,128)(2,1)} %get-tuple-element.20.res_ref) | copy-start | bytes 688132
  68.0 84.1 %copy-start = (bf16[128,7168]{1,0:T(8,128)(2,1)S(1)}, bf16[128,7168]{1,0:T(8,128)(2,1)}, u32[]{:S(2)}) copy-start(bf16[128,7168]{1,0:T(8,128)(2,1)} %get-tuple-element.13.q_hbm) | copy-start | bytes 5505028
  152.1 1.2 copy-start.2

commit v4 on v3

--- a/solution.py
+++ b/solution.py
@@ -94,9 +94,10 @@
         block(b, BLK)
         return carry
 
-    def first_half():
-        ranges()
-        lax.fori_loop(0, 4, early, 0)
+    def first_half(begin, end):
+        if begin == 0:
+            ranges()
+        lax.fori_loop(begin, end, early, 0)
 
     def later(step):
         if isinstance(step, int) and step == 3:
@@ -222,54 +223,43 @@
     return drain
 
 
-def attend(q_ref, latent_ref, up, spread, att_ref):
-    tokens, heads = q_ref.shape[0], q_ref.shape[1]
-    queries = q_ref[...].astype(F32)
-    spread[0] = queries[:, :, :NOPE].reshape(tokens * heads, NOPE)
-    blank = jnp.zeros((tokens, heads, NOPE - ROPE), F32)
-    spread[1] = jnp.concatenate([queries[:, :, NOPE:], blank], axis=2).reshape(
-        tokens * heads, NOPE
-    )
-    low = latent_ref[:, :LATENT]
-    rotary = jnp.concatenate(
-        [latent_ref[:, LATENT:].astype(F32), jnp.zeros((tokens, NOPE - ROPE), F32)], axis=1
-    ).astype(BF16)
+def attend(q_ref, latent_ref, up, att_ref):
+    heads, tokens = q_ref.shape[0], q_ref.shape[2]
+    rows = (((0,), (0,)), ((), ()))
+    low = latent_ref[:LATENT, :]
+    rotary = latent_ref[LATENT:, :]
     causal = lax.broadcasted_iota(jnp.int32, (tokens, tokens), 1) <= lax.broadcasted_iota(
         jnp.int32, (tokens, tokens), 0
     )
     for h in range(heads):
-        both = jnp.dot(low, up[h], preferred_element_type=F32).astype(BF16)
-        query = jnp.concatenate(
-            [spread[k, pl.ds(h, tokens, heads), :] for k in range(2)], axis=1
-        ).astype(BF16)
-        key = jnp.concatenate([both[:, :NOPE], rotary], axis=1)
-        scores = lax.dot_general(
-            query, key, (((1,), (1,)), ((), ())), preferred_element_type=F32
-        ) * (1.0 / math.sqrt(NOPE + ROPE))
+        both = lax.dot_general(up[h], low, rows, preferred_element_type=F32).astype(BF16)
+        key = jnp.concatenate([both[:NOPE], rotary], axis=0)
+        scores = lax.dot_general(q_ref[h], key, rows, preferred_element_type=F32) * (
+            1.0 / math.sqrt(NOPE + ROPE)
+        )
         scores = jnp.where(causal, scores, -1e30)
         expo = jnp.exp(scores - jnp.max(scores, axis=1, keepdims=True))
         probs = (expo / jnp.sum(expo, axis=1, keepdims=True)).astype(BF16)
-        att_ref[:, h * VHEAD:(h + 1) * VHEAD] = jnp.dot(
-            probs, both[:, NOPE:], preferred_element_type=F32
+        att_ref[:, h * VHEAD:(h + 1) * VHEAD] = lax.dot_general(
+            probs, both[NOPE:], (((1,), (1,)), ((), ())), preferred_element_type=F32
         ).astype(BF16)
 
 
 def route(ids_ref, num_ref, slot_ref, pick_ref, comb_ref):
-    tokens, experts_all = ids_ref.shape[0], slot_ref.shape[1]
+    tokens, experts_all = ids_ref.shape[1], slot_ref.shape[1]
     slots = pick_ref.shape[0] // CAP
-    names = lax.broadcasted_iota(jnp.int32, (tokens, experts_all), 1)
-    picks = jnp.zeros((tokens, experts_all), F32)
-    gates = jnp.zeros((tokens, experts_all), F32)
-    for k in range(ids_ref.shape[1]):
-        hit = ids_ref[:, k:k + 1] == names
+    names = lax.broadcasted_iota(jnp.int32, (experts_all, tokens), 0)
+    picks = jnp.zeros((experts_all, tokens), F32)
+    gates = jnp.zeros((experts_all, tokens), F32)
+    for k in range(ids_ref.shape[0]):
+        hit = ids_ref[k:k + 1, :] == names
         picks = jnp.where(hit, 1.0, picks)
-        gates = jnp.where(hit, num_ref[:, k:k + 1].astype(F32), gates)
+        gates = jnp.where(hit, num_ref[k:k + 1, :].astype(F32), gates)
     kept = jnp.where(
         slot_ref[...] == lax.broadcasted_iota(jnp.int32, (slots, experts_all), 0), 1.0, 0.0
     ).astype(BF16)
-    lanes = (((1,), (1,)), ((), ()))
-    slot_picks = lax.dot_general(kept, picks.astype(BF16), lanes, preferred_element_type=F32)
-    slot_gates = lax.dot_general(kept, gates.astype(BF16), lanes, preferred_element_type=F32)
+    slot_picks = jnp.dot(kept, picks.astype(BF16), preferred_element_type=F32)
+    slot_gates = jnp.dot(kept, gates.astype(BF16), preferred_element_type=F32)
     earlier = jnp.where(
         lax.broadcasted_iota(jnp.int32, (tokens, tokens), 0)
         < lax.broadcasted_iota(jnp.int32, (tokens, tokens), 1), 1.0, 0.0
@@ -289,7 +279,7 @@
     w_hbm, lift_hbm,
     out_ref, pick, comb, q_hbm,
     weight, lift, quant, wnat, cur, err, qi, lo, st, rs,
-    spread, att_own, proj, att, ring, fin, landed,
+    att_own, proj, att, ring, fin, landed,
     load_sem, proj_send, proj_recv, cross_send, cross_recv, att_send, att_recv,
     ring_send, ring_recv, fin_send, fin_recv,
 ):
@@ -381,7 +371,7 @@
     own_across.start()
 
     loads[0].wait()
-    attend(q_in_ref, latent_ref, lift, spread, att_own)
+    attend(q_in_ref, latent_ref, lift, att_own)
 
     own_a = [
         push(att_own, att.at[y], sems(att_send, att_recv, 0), y_up),
@@ -407,6 +397,11 @@
     proj[pl.ds(x * 2 + c, 1)] = proj_ref[...][None]
     att[pl.ds(y, 1)] = att_own[...][None]
     route(ids_ref, num_ref, slot_ref, pick, comb)
+    loads[1].wait()
+    quantize_first, quantize_later = quantize_panel(
+        us_ref, weight, u_ref, sel_ref, quant, wnat, cur, err, qi, lo, st, rs
+    )
+    quantize_first(0, 1)
     for k in range(2, 4):
         from_p[k].wait_recv()
     across(down_x, 1).start()
@@ -415,14 +410,11 @@
         copy.wait_recv()
     for copy in relay_a:
         copy.start()
-    loads[1].wait()
-    quantize_first, quantize_later = quantize_panel(
-        us_ref, weight, u_ref, sel_ref, quant, wnat, cur, err, qi, lo, st, rs
-    )
-    quantize_first()
+    quantize_first(1, 3)
     for copy in far_p:
         copy.wait_recv()
     across(far_x, 3).start()
+    quantize_first(3, 4)
     for copy in far_a:
         copy.wait_recv()
     for slot, k in enumerate((x, down_x, up_x, far_x)):
@@ -537,46 +529,7 @@
     ]
     for copy in loads:
         copy.start()
-    outgoing[...] = jnp.dot(pick[...], res_ref[...], preferred_element_type=F32).astype(BF16)
-    pl.semaphore_wait(pltpu.get_barrier_semaphore(), CHIPS + RING - 1)
-
     unit = 2 * CAP
-
-    def exchange(src, dst, send, recv, meanwhile):
-        def rows_of(k):
-            return pl.ds(pl.multiple_of(k * unit, unit), unit)
-
-        def out(k):
-            to = chip_at(k)
-            return push(
-                src.at[rows_of(to)], dst.at[rows_of(chip)], (send.at[k], recv.at[k]),
-                (to * 2 + c, z),
-            )
-
-        def come(k):
-            here = dst.at[rows_of(chip_at(CHIPS - k))]
-            return push(here, here, (send.at[k], recv.at[k]), (chip_at(k) * 2 + c, z))
-
-        def start(k, carry):
-            out(k).start()
-            return carry
-
-        def arrive(k, carry):
-            come(k).wait_recv()
-            return carry
-
-        def leave(k, carry):
-            out(k).wait_send()
-            return carry
-
-        lax.fori_loop(1, CHIPS, start, 0)
-        dst[rows_of(chip), :] = src[rows_of(chip), :]
-        meanwhile()
-        lax.fori_loop(1, CHIPS, arrive, 0)
-        return leave
-
-    leave_out = exchange(outgoing, incoming, out_send, out_recv, lambda: None)
-
     count = CHIPS * unit
     half = count // 2
     r = lax.broadcasted_iota(jnp.int32, (count, count), 0)
@@ -585,6 +538,44 @@
     by_core = (q == spot).astype(F32).astype(BF16)
     spot_back = ((q >> 3) & 15) * unit + (((q >> 7) ^ c) & 1) * CAP + (q & 7)
     by_chip = (r == spot_back).astype(F32).astype(BF16)
+
+    outgoing[...] = jnp.dot(pick[...], res_ref[...], preferred_element_type=F32).astype(BF16)
+    pl.semaphore_wait(pltpu.get_barrier_semaphore(), CHIPS + RING - 1)
+
+    def exchange(src, dst, send, recv, meanwhile):
+        def rows_of(k):
+            return pl.ds(pl.multiple_of(k * unit, unit), unit)
+
+        def out(k):
+            to = chip_at(k)
+            return push(
+                src.at[rows_of(to)], dst.at[rows_of(chip)], (send.at[k], recv.at[k]),
+                (to * 2 + c, z),
+            )
+
+        def come(k):
+            here = dst.at[rows_of(chip_at(CHIPS - k))]
+            return push(here, here, (send.at[k], recv.at[k]), (chip_at(k) * 2 + c, z))
+
+        def start(k, carry):
+            out(k).start()
+            return carry
+
+        def arrive(k, carry):
+            come(k).wait_recv()
+            return carry
+
+        def leave(k, carry):
+            out(k).wait_send()
+            return carry
+
+        lax.fori_loop(1, CHIPS, start, 0)
+        dst[rows_of(chip), :] = src[rows_of(chip), :]
+        meanwhile()
+        lax.fori_loop(1, CHIPS, arrive, 0)
+        return leave
+
+    leave_out = exchange(outgoing, incoming, out_send, out_recv, lambda: None)
 
     both = jnp.dot(by_core, incoming[...], preferred_element_type=F32).astype(BF16)
     raw[0:half, :] = both[:half]
@@ -708,7 +699,6 @@
     dma = pltpu.SemaphoreType.DMA
     columns, depth = projection.shape
     tokens, block = residual.shape
-    heads = queries.shape[1]
     rows = 2 * CAP * CHIPS
     meet = (2, 2, 2, RING // 2)
     return pl.pallas_call(
@@ -732,7 +722,6 @@
             pltpu.VMEM((tiles, NSUB, LANES), F32),
             pltpu.VMEM((tiles, NSUB, LANES), F32),
             pltpu.VMEM((tiles, NSUB, LANES), F32),
-            pltpu.VMEM((2, tokens * heads, NOPE), F32),
             pltpu.VMEM((tokens, depth), BF16),
             pltpu.VMEM((2 * SIDE, columns, depth), BF16),
             pltpu.VMEM((SIDE, tokens, depth), BF16),
@@ -813,8 +802,8 @@
     inv_chol,
 ):
     residual_out, pick_any, combine, quantized = front(
-        inv_chol[0], out_proj.T, residual_in, queries, latent, expert_ids, gate_num,
-        slot_table[None], down_proj[0], latent_up,
+        inv_chol[0], out_proj.T, residual_in, queries.transpose(1, 2, 0), latent.T, expert_ids.T,
+        gate_num.T, slot_table[None], down_proj[0], latent_up,
     )
     moe, gram = back(
         residual_out, norm_gain[None], pick_any, combine, gate_proj[0], up_proj[0], quantized

time: 154 us -> 144 us (0.935)
  local copies, waits for them, and re-layouts: 12.2 us -> 5.47 us
  Pallas kernels: 141 us -> 138 us
    unnamed x14 -> x10, local copies, waits for them, and re-layouts: 10.9 us -> 4.2 us
    pallas_call x1, Pallas kernels: 59.4 us -> 57.4 us  [front(): pl.pallas_call(front_kernel, out_shape=(jax.ShapeDtypeStruct((tokens, blo...]
where the time goes in v4:
time: 144 us
  Pallas kernels  138 us (96%)
  local copies, waits for them, and re-layouts  5.47 us (4%)
    pallas_call x1, Pallas kernels, back(): pl.pallas_call(back_kernel, out_shape=(jax.ShapeDtypeStruct((tokens, bloc...  80.5 us
    pallas_call x1, Pallas kernels, front(): pl.pallas_call(front_kernel, out_shape=(jax.ShapeDtypeStruct((tokens, blo...  57.4 us
    unnamed x10, local copies, waits for them, and re-layouts  4.2 us

profile of v4, /device:TPU:1, one launch (start us, length us, event | category | flops | bytes accessed | tf_op | source)
XLA Modules:
  0.0 144.0 jit_solution(17199956443340693200)
XLA Ops:
  0.6 1.3 broadcast_in_dim.13.gain_ref
  1.9 57.4 %front.1 = (bf16[128,896]{1,0:T(8,128)(2,1)}, bf16[256,128]{1,0:T(8,128)(2,1)}, bf16[256,128]{1,0:T(8,128)(2,1)}, bf16[128,7168]{1,0:T(8,128)(2,1)}) custom-call(f32[128,128]{1,0:T(8,128)} %bitcast.18, f32[128,128]{1,0:T(8,128)} %bitcast.19, bf16[48,128]{1,0:T(8,128)(2,1)} %constant.2.clone.sel_ref, bf16[224,1024]{1,0:T(8,128)(2,1)} %bitcast.16, ...), custom_call_target="tpu_custom_call" | custom-call | tf_op jit(solution)/shard_map/front/pallas_call | solution.py:704
  59.3 0.0 copy-start.1
  59.3 0.0 copy-start
  59.3 80.5 %back.1 = (bf16[128,896]{1,0:T(8,128)(2,1)}, f32[128,128]{1,0:T(8,128)}) custom-call(bf16[128,896]{1,0:T(8,128)(2,1)} %get-tuple-element.20.res_ref, bf16[1,896]{1,0:T(2,128)(2,1)} %broadcast_in_dim.13.gain_ref, bf16[256,128]{1,0:T(8,128)(2,1)} %get-tuple-element.11.pick, bf16[256,128]{1,0:T(8,128)(2,1)} %get-tuple-element.12.comb, ...), custom_call_target="tpu_custom_call" | custom-call | tf_op jit(solution)/shard_map/back/pallas_call | solution.py:754
  139.8 0.0 copy-done.1
  139.8 0.7 copy.22
  140.5 1.6 %copy.23 = bf16[128,896]{1,0:T(8,128)(2,1)} copy(bf16[128,896]{1,0:T(8,128)(2,1)} %get-tuple-element.21) | data formatting | bytes 458752
  142.2 0.0 copy-done
  142.2 0.0 copy-start.2
  142.2 1.2 copy.24
  143.4 0.0 copy-done.2
  143.4 0.6 copy.25
Async XLA Ops:
  59.3 80.6 %copy-start.1 = (bf16[128,896]{1,0:T(8,128)(2,1)S(1)}, bf16[128,896]{1,0:T(8,128)(2,1)}, u32[]{:S(2)}) copy-start(bf16[128,896]{1,0:T(8,128)(2,1)} %get-tuple-element.20.res_ref) | copy-start | bytes 688132
  59.3 82.9 %copy-start = (bf16[128,7168]{1,0:T(8,128)(2,1)S(1)}, bf16[128,7168]{1,0:T(8,128)(2,1)}, u32[]{:S(2)}) copy-start(bf16[128,7168]{1,0:T(8,128)(2,1)} %get-tuple-element.13.q_hbm) | copy-start | bytes 5505028
  142.2 1.2 copy-start.2

commit v5 on v4

--- a/solution.py
+++ b/solution.py
@@ -197,7 +197,7 @@
 
     lax.fori_loop(1, RING // 2 - 1, middle, 0)
     advance(RING // 2 - 1, streams[:2])
-    for half in range(2):
+    for half in (1, 0):
         own = partial(z, half)
         for sub in range(2):
             value = rows(own, sub)
@@ -577,11 +577,14 @@
 
     leave_out = exchange(outgoing, incoming, out_send, out_recv, lambda: None)
 
-    both = jnp.dot(by_core, incoming[...], preferred_element_type=F32).astype(BF16)
-    raw[0:half, :] = both[:half]
-    crossing[...] = both[half:]
+    crossing[...] = jnp.dot(
+        by_core[half:], incoming[...], preferred_element_type=F32
+    ).astype(BF16)
     over = push(crossing, raw.at[pl.ds(half, half)], (sib_send.at[0], sib_recv.at[0]), sibling)
     over.start()
+    raw[0:half, :] = jnp.dot(
+        by_core[:half], incoming[...], preferred_element_type=F32
+    ).astype(BF16)
     over.wait_recv()
 
     wide = raw[...].astype(F32)
@@ -641,9 +644,6 @@
     gate = jnp.concatenate([sums[0, 0], sums[0, 1]], axis=0) * scale
     up = jnp.concatenate([sums[1, 0], sums[1, 1]], axis=0) * scale
     hidden[...] = (gate / (1.0 + jnp.exp(-gate)) * up).astype(BF16)
-    gram_ref[...] = lax.dot_general(
-        hidden[...], hidden[...], (((0,), (0,)), ((), ())), preferred_element_type=F32
-    ) / count
 
 
     def partial_b(goal, side):
@@ -658,26 +658,34 @@
             hidden[begin:begin + quarter, :], quant[goal], preferred_element_type=F32
         )
 
+    def home(sub):
+        return push(
+            rows_out.at[pl.ds(sub * quarter, quarter)],
+            gathered.at[pl.ds(half + sub * quarter, quarter)],
+            (sib_send.at[1 + sub], sib_recv.at[1 + sub]), sibling,
+        )
+
     def finish_b(side, sub, value):
         if side == 0:
             gathered[sub * quarter:(sub + 1) * quarter, :] = value.astype(BF16)
         else:
             rows_out[sub * quarter:(sub + 1) * quarter, :] = value.astype(BF16)
+            home(sub).start()
 
     for copy in loads[2:]:
         copy.wait()
     drain_b = ring_sum(z, at, ring_b, b_send, b_recv, partial_b, rows_b, finish_b)
 
 
-    home = push(
-        rows_out, gathered.at[pl.ds(half, half)], (sib_send.at[1], sib_recv.at[1]), sibling
-    )
-    home.start()
-    home.wait_recv()
+    for sub in range(2):
+        home(sub).wait_recv()
     returning[...] = jnp.dot(
         by_chip, gathered[...], preferred_element_type=F32
     ).astype(BF16)
     def settle():
+        gram_ref[...] = lax.dot_general(
+            hidden[...], hidden[...], (((0,), (0,)), ((), ())), preferred_element_type=F32
+        ) / count
         drain_a()
         drain_b()
         lax.fori_loop(1, CHIPS, leave_out, 0)
@@ -689,7 +697,8 @@
     ).astype(BF16)
 
     over.wait_send()
-    home.wait_send()
+    for sub in range(2):
+        home(sub).wait_send()
     lax.fori_loop(1, CHIPS, leave_back, 0)
 def front(us, projection, residual, queries, latent, ids, num, slots, weight, lift):
     width = weight.shape[1]
@@ -775,7 +784,7 @@
             pltpu.VMEM(wide, BF16),
             pltpu.VMEM(wide, BF16),
             pltpu.VMEM(wide, BF16),
-            dma((2 + NSUB,)), dma((CHIPS,)), dma((CHIPS,)), dma((2,)), dma((2,)), dma((RING,)),
+            dma((2 + NSUB,)), dma((CHIPS,)), dma((CHIPS,)), dma((3,)), dma((3,)), dma((RING,)),
             dma((RING,)), dma(meet), dma(meet), dma(meet), dma(meet), dma((CHIPS,)),
             dma((CHIPS,)),
         ],

time: 144 us -> 144 us (level)
    pallas_call x1, Pallas kernels: 57.4 us -> 53.6 us  [front(): pl.pallas_call(front_kernel, out_shape=(jax.ShapeDtypeStruct((tokens, blo...]
    pallas_call x1, Pallas kernels: 80.5 us -> 83.7 us  [back(): pl.pallas_call(back_kernel, out_shape=(jax.ShapeDtypeStruct((tokens, bloc...]
where the time goes in v5:
time: 144 us
  Pallas kernels  137 us (95%)
  local copies, waits for them, and re-layouts  5.47 us (4%)
    pallas_call x1, Pallas kernels, back(): pl.pallas_call(back_kernel, out_shape=(jax.ShapeDtypeStruct((tokens, bloc...  83.7 us
    pallas_call x1, Pallas kernels, front(): pl.pallas_call(front_kernel, out_shape=(jax.ShapeDtypeStruct((tokens, blo...  53.6 us
    unnamed x10, local copies, waits for them, and re-layouts  4.2 us

profile of v5, /device:TPU:1, one launch (start us, length us, event | category | flops | bytes accessed | tf_op | source)
XLA Modules:
  0.0 143.5 jit_solution(8225495092656585238)
XLA Ops:
  0.6 1.3 broadcast_in_dim.13.gain_ref
  1.9 53.6 %front.1 = (bf16[128,896]{1,0:T(8,128)(2,1)}, bf16[256,128]{1,0:T(8,128)(2,1)}, bf16[256,128]{1,0:T(8,128)(2,1)}, bf16[128,7168]{1,0:T(8,128)(2,1)}) custom-call(f32[128,128]{1,0:T(8,128)} %bitcast.18, f32[128,128]{1,0:T(8,128)} %bitcast.19, bf16[48,128]{1,0:T(8,128)(2,1)} %constant.2.clone.sel_ref, bf16[224,1024]{1,0:T(8,128)(2,1)} %bitcast.16, ...), custom_call_target="tpu_custom_call" | custom-call | tf_op jit(solution)/shard_map/front/pallas_call | solution.py:713
  55.5 0.0 copy-start.1
  55.6 0.0 copy-start
  55.6 83.7 %back.1 = (bf16[128,896]{1,0:T(8,128)(2,1)}, f32[128,128]{1,0:T(8,128)}) custom-call(bf16[128,896]{1,0:T(8,128)(2,1)} %get-tuple-element.20.res_ref, bf16[1,896]{1,0:T(2,128)(2,1)} %broadcast_in_dim.13.gain_ref, bf16[256,128]{1,0:T(8,128)(2,1)} %get-tuple-element.11.pick, bf16[256,128]{1,0:T(8,128)(2,1)} %get-tuple-element.12.comb, ...), custom_call_target="tpu_custom_call" | custom-call | tf_op jit(solution)/shard_map/back/pallas_call | solution.py:763
  139.3 0.0 copy-done.1
  139.3 0.7 copy.22
  140.0 1.6 %copy.23 = bf16[128,896]{1,0:T(8,128)(2,1)} copy(bf16[128,896]{1,0:T(8,128)(2,1)} %get-tuple-element.21) | data formatting | bytes 458752
  141.7 0.0 copy-done
  141.7 0.0 copy-start.2
  141.7 1.2 copy.24
  142.9 0.0 copy-done.2
  142.9 0.6 copy.25
Async XLA Ops:
  55.5 83.8 %copy-start.1 = (bf16[128,896]{1,0:T(8,128)(2,1)S(1)}, bf16[128,896]{1,0:T(8,128)(2,1)}, u32[]{:S(2)}) copy-start(bf16[128,896]{1,0:T(8,128)(2,1)} %get-tuple-element.20.res_ref) | copy-start | bytes 688132
  55.6 86.1 %copy-start = (bf16[128,7168]{1,0:T(8,128)(2,1)S(1)}, bf16[128,7168]{1,0:T(8,128)(2,1)}, u32[]{:S(2)}) copy-start(bf16[128,7168]{1,0:T(8,128)(2,1)} %get-tuple-element.13.q_hbm) | copy-start | bytes 5505028
  141.7 1.2 copy-start.2
